TPU v7x, 32 devices: a whole 2x2x4 slice. The times are simulated.
32 devices in a mesh: groups: 2 (over x), fsdp: 16 (over z, y, core).
Axes of the slice: x: 2, y: 2, z: 4, core: 2. Of those that a mesh axis runs over, the one named last changes fastest.
Arguments:
- tokens: bfloat16 [8192, 8192], P(('groups', 'fsdp')), parts along dimension 0, may hold values from -6 to 6
- key_weight: bfloat16 [8192, 1024], P('fsdp'), may hold values from -0.0625 to 0.0625
- adapter_down: bfloat16 [16384, 256], P(('groups', 'fsdp')), parts along dimension 0, may hold values from -0.0625 to 0.0625
- adapter_up: bfloat16 [512, 1024], P(('groups', 'fsdp')), parts along dimension 0, may hold values from -0.75 to 0.75
- key_cotangent: bfloat16 [8192, 1024], P(('groups', 'fsdp')), parts along dimension 0, may hold values from -6 to 6
- block_job: int32 [64], P('groups'), parts along dimension 0, may hold values from 0 to 3
- block_live: int32 [64], P(('groups', 'fsdp')), parts along dimension 0, may hold values from 1 to 128, as said below
- job_rank: int32 [8], P('groups'), parts along dimension 0, may hold values from 16 to 64, as said below
Outputs:
- keys: bfloat16 [8192, 1024], P(('groups', 'fsdp')), parts along dimension 0
- input_grad: bfloat16 [8192, 8192], P(('groups', 'fsdp')), parts along dimension 0
- down_grad: float32 [16384, 256], P(('groups', 'fsdp')), parts along dimension 0
- up_grad: float32 [512, 1024], P(('groups', 'fsdp')), parts along dimension 0
There are 2 independent parts, one for each index of `groups`. A program takes and returns all parts, laid end to end along the dimension named above; an argument that names none is the same for every part. Nothing has to cross between parts.
Inputs may be any that keep to these rules, and one draw needn't show every extreme that they name: `block_live`: one block is full in every draw. `job_rank`: each rank is 16, 32 or 64; some job has rank 64 and some job rank 16.
All inputs are finite; a program needn't handle non-finite values.
Results may differ from a plain program's by a relative error of at most 0.0029.
Values may be sent and summed in bfloat16 or wider, within the bound.
No kernel may reach another device: no remote copies, remote signals or barrier semaphores. Data moves between devices by JAX's collectives and lax.ppermute only.
A program may use at most 128 MiB of HBM per device.

v0:
```python
import jax
import jax.numpy as jnp
from jax import lax
from jax.sharding import PartitionSpec as P

RANK = 64
BLOCK = 128


def per_device(
    tokens, key_weight, adapter_down, adapter_up, key_cotangent, block_job, block_live, job_rank
):
    tok_count = tokens.shape[0]
    jobs_here = job_rank.shape[0]
    width_low = adapter_down.shape[1]
    blocks_here = block_live.shape[0]
    my_index = lax.axis_index("fsdp")
    local_job = lax.dynamic_slice_in_dim(block_job, my_index * blocks_here, blocks_here, 0)
    weight_full, down_full = (
        lax.all_gather(key_weight, "fsdp", axis=0, tiled=True),
        lax.all_gather(adapter_down, "fsdp", axis=0, tiled=True),
    )
    up_full = lax.all_gather(adapter_up, "fsdp", axis=0, tiled=True)
    onehot = (local_job[:, None] == jnp.arange(jobs_here, dtype=jnp.int32)[None, :]).astype(
        jnp.float32
    )
    local_count = jnp.sum(onehot * block_live[:, None].astype(jnp.float32), axis=0)
    count = lax.psum(local_count, "fsdp")
    position = jnp.arange(tok_count, dtype=jnp.int32)
    tok_job = jnp.repeat(local_job, BLOCK)
    tok_live = jnp.repeat(block_live, BLOCK)
    live = (position % BLOCK < tok_live).astype(jnp.float32)
    columns = jnp.arange(width_low, dtype=jnp.int32)
    col_job = columns // RANK
    col_rank = jnp.repeat(job_rank, RANK)
    col_scale = jnp.where(columns % RANK < col_rank, 16.0 / col_rank.astype(jnp.float32), 0.0)
    colmask = (
        (col_job[None, :] == tok_job[:, None]).astype(jnp.float32)
        * col_scale[None, :]
        * live[:, None]
    )
    low = (jnp.dot(tokens, down_full, preferred_element_type=jnp.float32) * colmask).astype(
        jnp.bfloat16
    )
    keys_full = jnp.dot(tokens, weight_full, preferred_element_type=jnp.float32) + jnp.dot(
        low, up_full, preferred_element_type=jnp.float32
    )
    keys = (keys_full * live[:, None]).astype(jnp.bfloat16)
    grad_keys = (key_cotangent.astype(jnp.float32) * live[:, None]).astype(jnp.bfloat16)
    grad_low = (jnp.dot(grad_keys, up_full.T, preferred_element_type=jnp.float32) * colmask).astype(
        jnp.bfloat16
    )
    input_grad = (
        jnp.dot(grad_keys, weight_full.T, preferred_element_type=jnp.float32)
        + jnp.dot(grad_low, down_full.T, preferred_element_type=jnp.float32)
    ).astype(jnp.bfloat16)
    norm = jnp.repeat(1.0 / jnp.sqrt(jnp.maximum(count, 1.0)), RANK)
    contract = (((0,), (0,)), ((), ()))
    compact = jnp.sum(
        grad_low.astype(jnp.float32).reshape(tok_count, jobs_here, RANK), axis=1
    ).astype(jnp.bfloat16)
    compact_all = lax.all_gather(compact, "fsdp", axis=0, tiled=True)
    features = lax.all_to_all(tokens, "fsdp", split_axis=1, concat_axis=0, tiled=True)
    every_job = jnp.repeat(block_job, BLOCK)
    pieces = []
    for job_index in range(jobs_here):
        selected = compact_all * (every_job == job_index).astype(jnp.bfloat16)[:, None]
        pieces.append(
            lax.dot_general(features, selected, contract, preferred_element_type=jnp.float32)
        )
    owned = jnp.concatenate(pieces, axis=1)
    down_grad = owned * norm[None, :]
    up_term = lax.dot_general(low, grad_keys, contract, preferred_element_type=jnp.float32)
    up_owned = lax.psum_scatter(up_term, "fsdp", scatter_dimension=0, tiled=True)
    up_rows_here = adapter_up.shape[0]
    norm_rows = lax.dynamic_slice_in_dim(norm, my_index * up_rows_here, up_rows_here, 0)
    up_grad = up_owned * norm_rows[:, None]
    return (keys, input_grad, down_grad, up_grad)


def solution(mesh):
    placed = (
        P(("groups", "fsdp"), None),
        P("fsdp", None),
        P(("groups", "fsdp"), None),
        P(("groups", "fsdp"), None),
        P(("groups", "fsdp"), None),
        P("groups"),
        P(("groups", "fsdp")),
        P("groups"),
    )
    return jax.shard_map(
        per_device,
        mesh=mesh,
        in_specs=placed,
        out_specs=(
            P(("groups", "fsdp"), None),
            P(("groups", "fsdp"), None),
            P(("groups", "fsdp"), None),
            P(("groups", "fsdp"), None),
        ),
        check_vma=False,
    )
```

profile of v0, /device:TPU:0, one launch (start us, length us, event | category | flops | bytes accessed | tf_op | source)
XLA Modules:
  0.0 346.2 jit_solution(3946998746982313695)
XLA Ops:
  7.2 0.7 all-gather.5.cloned.1.call-update
  8.0 0.7 broadcast_in_dim.39
  8.8 0.7 dynamic_slice.6
  9.5 0.7 compare_convert_fusion.4
  10.3 53.2 %all-gather.5.cloned.1.call-done = bf16[8192,256]{1,0:T(8,128)(2,1)} async-done(((bf16[512,256]{1,0:T(8,128)(2,1)}), bf16[8192,256]{1,0:T(8,128)(2,1)}) %all-gather.5.cloned.1.call-update) | async-done | bytes 4194320 | tf_op jit(solution)/shard_map/all_gather | solution.py:21
  63.5 4.7 %fusion.3 = bf16[256,256]{1,0:T(8,128)(2,1)S(1)} fusion(bf16[256,8192]{1,0:T(8,128)(2,1)} %param.8, bf16[8192,256]{1,0:T(8,128)(2,1)} %all-gather.5.cloned.1.call-done, f32[256]{0:T(256)S(1)} %compare_convert_fusion.4, f32[256]{0:T(256)S(1)} %compare_select_fusion.1, s32[256]{0:T(256)S(1)} %and_select_fusion.2, s32[256]{0:T(256)S(1)} %broadcast_bitcast_fusion.4), kind=kOutput, calls=%fused_computation.7 | convolution fusion | flops 1074069504 | bytes 8523776 | tf_op jit(solution)/shard_map/dot_general | solution.py:42
  68.2 1.4 fusion.16
  69.6 0.7 all-gather.3.cloned.1.call-update
  70.3 6.4 %copy.29 = bf16[256,8192]{0,1:T(8,128)(2,1)} copy(bf16[256,8192]{1,0:T(8,128)(2,1)} %param.8) | data formatting | bytes 8388608 | tf_op args[0]
  76.7 4.7 %all-to-all-start = ((bf16[256,16,512]{0,2,1:T(8,128)(2,1)}), bf16[256,16,512]{0,2,1:T(8,128)(2,1)}, u32[]{:S(2)}, u32[]{:S(2)}) async-start(bf16[256,16,512]{0,2,1:T(8,128)(2,1)} %bitcast.43), calls=%async_computation | async-start | bytes 8388608 | tf_op jit(solution)/shard_map/all_to_all | solution.py:63
  81.5 102.6 %psum.7 = f32[4]{0:T(128)S(1)} all-reduce(f32[4]{0:T(128)S(1)} %fusion.15), channel_id=1, replica_groups=mesh['groups'=2,'fsdp'=16] {'fsdp'}, use_global_device_ids=true, to_apply=%region_2.3 | all-reduce | flops 4 | bytes 32 | tf_op jit(solution)/shard_map/psum | solution.py:28
  184.1 35.1 %all_gather.14 = bf16[256,1024]{1,0:T(8,128)(2,1)S(1)} all-gather(bf16[16,1024]{1,0:T(8,128)(2,1)S(1)} %copy-done.4), channel_id=1, replica_groups=mesh['groups'=2,'fsdp'=16] {'fsdp'}, dimensions={0}, use_global_device_ids=true | all-gather | bytes 557056 | tf_op jit(solution)/shard_map/all_gather | solution.py:23
  220.1 24.0 %all_gather.15 = bf16[4096,64]{0,1:T(8,128)(2,1)S(1)} all-gather(bf16[256,64]{0,1:T(8,128)(2,1)S(1)} %reduce), channel_id=1, replica_groups=mesh['groups'=2,'fsdp'=16] {'fsdp'}, dimensions={0}, use_global_device_ids=true | all-gather | bytes 557056 | tf_op jit(solution)/shard_map/all_gather | solution.py:62
  244.1 6.4 %copy.30 = bf16[16,256,512]{2,1,0:T(8,128)(2,1)} copy(bf16[16,256,512]{1,2,0:T(8,128)(2,1)} %bitcast.5) | data formatting | bytes 8388608 | tf_op jit(solution)/shard_map/all_to_all | solution.py:63
  250.5 3.2 convolution_bitcast_fusion
  253.9 0.8 convolution_bitcast_fusion.1
  254.8 0.8 convolution_bitcast_fusion.2
  255.6 0.8 convolution_bitcast_fusion.3
  256.6 1.0 copy.31
  257.9 1.5 broadcast_multiply_fusion
  259.5 45.3 %all-gather.3.cloned.1.call-done = bf16[8192,1024]{1,0:T(8,128)(2,1)} async-done(((bf16[512,1024]{1,0:T(8,128)(2,1)}), bf16[8192,1024]{1,0:T(8,128)(2,1)}) %all-gather.3.cloned.1.call-update) | async-done | bytes 16777232 | tf_op jit(solution)/shard_map/all_gather | solution.py:20
  304.8 19.1 %fusion.17 = f32[256,8192]{1,0:T(8,128)} fusion(bf16[8192,1024]{1,0:T(8,128)(2,1)} %all-gather.3.cloned.1.call-done, bf16[256,1024]{1,0:T(8,128)(2,1)S(1)} %copy-done.3, f32[256]{0:T(256)S(1)} %compare_convert_fusion.4), kind=kOutput, calls=%fused_computation.48 | convolution fusion | flops 4295753728 | bytes 25691136 | tf_op jit(solution)/shard_map/dot_general | solution.py:54
  323.9 12.5 %fusion.2 = bf16[256,1024]{1,0:T(8,128)(2,1)} fusion(f32[256,1024]{1,0:T(8,128)S(1)} %fusion.18, bf16[256,8192]{1,0:T(8,128)(2,1)} %param.8, bf16[8192,1024]{1,0:T(8,128)(2,1)} %all-gather.3.cloned.1.call-done, f32[256]{0:T(256)S(1)} %compare_convert_fusion.4), kind=kOutput, calls=%fused_computation.4 | convolution fusion | flops 4295753728 | bytes 22545408 | tf_op jit(solution)/shard_map/dot_general | solution.py:45
  336.3 3.4 fusion
  (38 shorter events, 2.0 us)
Async XLA Ops:
  7.2 56.3 %all-gather.5.cloned.1.call-start = ((), (), s32[]{:S(2)}) async-start(), calls=%async_computation.3 | async-start | bytes 4456448 | tf_op jit(solution)/shard_map/all_gather | solution.py:21
  7.9 250.0 %reduce-scatter.2.cloned.1.call-start = ((), (), s32[]{:S(2)}) async-start(), calls=%async_computation.4 | async-start | bytes 1114112 | tf_op jit(solution)/shard_map/reduce_scatter | solution.py:74
  10.3 57.9 %copy-start.3 = (bf16[256,1024]{1,0:T(8,128)(2,1)S(1)}, bf16[256,1024]{1,0:T(8,128)(2,1)}, u32[]{:S(2)}) copy-start(bf16[256,1024]{1,0:T(8,128)(2,1)} %param.12) | copy-start | bytes 1572868
  69.6 235.2 %all-gather.3.cloned.1.call-start = ((), (), s32[]{:S(2)}) async-start(), calls=%async_computation.2 | async-start | bytes 17825792 | tf_op jit(solution)/shard_map/all_gather | solution.py:20
  76.7 4.7 %copy-start.6 = (s32[2]{0:T(128)S(1)}, s32[2]{0:T(128)}, u32[]{:S(2)}) copy-start(s32[2]{0:T(128)} %param.14) | copy-start | bytes 28
  76.7 107.4 %copy-start.4 = (bf16[16,1024]{1,0:T(8,128)(2,1)S(1)}, bf16[16,1024]{1,0:T(8,128)(2,1)}, u32[]{:S(2)}) copy-start(bf16[16,1024]{1,0:T(8,128)(2,1)} %param.11) | copy-start | bytes 98308
  76.7 143.3 %copy-start.5 = (s32[32]{0:T(128)S(1)}, s32[32]{0:T(128)}, u32[]{:S(2)}) copy-start(s32[32]{0:T(128)} %param.13) | copy-start | bytes 388
  76.7 167.4 %all-to-all-start = ((bf16[256,16,512]{0,2,1:T(8,128)(2,1)}), bf16[256,16,512]{0,2,1:T(8,128)(2,1)}, u32[]{:S(2)}, u32[]{:S(2)}) async-start(bf16[256,16,512]{0,2,1:T(8,128)(2,1)} %bitcast.43), calls=%async_computation | async-start | bytes 8388608 | tf_op jit(solution)/shard_map/all_to_all | solution.py:63
  250.5 3.4 copy-start
  323.8 12.5 %copy-start.1 = (f32[256,8192]{1,0:T(8,128)S(1)}, f32[256,8192]{1,0:T(8,128)}, u32[]{:S(2)}) copy-start(f32[256,8192]{1,0:T(8,128)} %fusion.17) | copy-start | bytes 25165828
  323.9 12.5 %copy-start.2 = (bf16[8192,256]{1,0:T(8,128)(2,1)S(1)}, bf16[8192,256]{1,0:T(8,128)(2,1)}, u32[]{:S(2)}) copy-start(bf16[8192,256]{1,0:T(8,128)(2,1)} %all-gather.5.cloned.1.call-done) | copy-start | bytes 12582916
Sparse Core Ops, SparseCore 0:
  10.2 53.2 all-gather.4
  69.7 94.0 reduce-scatter.1
  166.1 138.5 all-gather.2
where the time goes:
time: 347 us; the launch traced here: 346 us
  blocking collectives  162 us (47%)
  waiting for transfers between devices  99.9 us (29%)
  matrix products  47.3 us (14%)
  local copies, waits for them, and re-layouts  16.2 us (5%)
  between operations  13.9 us (4%)
  starting transfers between devices  4.81 us (1%)
    psum x1, blocking collectives, per_device(): count = lax.psum(local_count, 'fsdp')  103 us
    all_gather x1, waiting for transfers between devices, per_device(): lax.all_gather(adapter_down, 'fsdp', axis=0, tiled=True)  53.2 us
    all_gather x1, waiting for transfers between devices, per_device(): lax.all_gather(key_weight, 'fsdp', axis=0, tiled=True)  45.3 us
    all_gather x1, blocking collectives, per_device(): up_full = lax.all_gather(adapter_up, 'fsdp', axis=0, tiled=True)  35.1 us
    all_gather x1, blocking collectives, per_device(): compact_all = lax.all_gather(compact, 'fsdp', axis=0, tiled=True)  24 us
    dot_general x1, matrix products, per_device(): jnp.dot(grad_keys, weight_full.T, preferred_element_type=jnp.float32)  19.1 us
    dot_general x1, matrix products, per_device(): jnp.dot(tokens, weight_full, preferred_element_type=jnp.float32)  12.5 us
    unnamed x16, local copies, waits for them, and re-layouts  7.67 us
  transfers between devices with their start and end apart: 4, of which 2 were waited for; matrix products, arithmetic and copies ran while one was open for 7% of the time, Pallas kernels for 0%

commit v1 on v0

--- a/solution.py
+++ b/solution.py
@@ -1,13 +1,168 @@
+import functools
+
 import jax
 import jax.numpy as jnp
 from jax import lax
+from jax.experimental import pallas as pl
+from jax.experimental.pallas import tpu as pltpu
 from jax.sharding import PartitionSpec as P
 
 RANK = 64
 BLOCK = 128
 
 
-def per_device(
+NT = (((1,), (1,)), ((), ()))
+TN = (((0,), (0,)), ((), ()))
+
+
+def pick_kernel(where, src, out):
+    out[...] = src[...]
+
+
+def pick_columns(where, tokens, shard):
+    count = tokens.shape[0]
+    blocks = where.shape[0]
+    return pl.pallas_call(
+        pick_kernel,
+        grid_spec=pltpu.PrefetchScalarGridSpec(
+            num_scalar_prefetch=1,
+            grid=(blocks,),
+            in_specs=[pl.BlockSpec((count, shard), lambda i, w: (0, w[i]))],
+            out_specs=pl.BlockSpec((count, shard), lambda i, w: (0, i)),
+        ),
+        out_shape=jax.ShapeDtypeStruct((count, blocks * shard), tokens.dtype),
+        cost_estimate=pl.CostEstimate(
+            flops=0, bytes_accessed=4 * count * blocks * shard, transcendentals=0
+        ),
+    )(where, tokens)
+
+
+def part_kernel(where, mine, theirs, low_mine, low_theirs, *refs):
+    total = lax.dot_general(mine[...], low_mine[...], TN, preferred_element_type=jnp.float32)
+    total += lax.dot_general(theirs[...], low_theirs[...], TN, preferred_element_type=jnp.float32)
+    if len(refs) == 2:
+        total += refs[0][...].astype(jnp.float32)
+    refs[-1][...] = total.astype(refs[-1].dtype)
+
+
+def part_sums(where, first, tokens, pair_tokens, low_mine, low_theirs, shard, received=None):
+    count = tokens.shape[0]
+    blocks = where.shape[0]
+    low_width = low_mine.shape[1]
+    whole = pl.BlockSpec((count, low_width), lambda i, w: (0, 0))
+    rows = pl.BlockSpec((shard, low_width), lambda i, w: (i, 0))
+    operands = [tokens, pair_tokens, low_mine, low_theirs]
+    specs = [
+        pl.BlockSpec((count, shard), lambda i, w: (0, w[i])),
+        pl.BlockSpec((count, shard), lambda i, w: (0, first + i)),
+        whole,
+        whole,
+    ]
+    if received is not None:
+        operands.append(received)
+        specs.append(rows)
+    return pl.pallas_call(
+        part_kernel,
+        grid_spec=pltpu.PrefetchScalarGridSpec(
+            num_scalar_prefetch=1, grid=(blocks,), in_specs=specs, out_specs=rows
+        ),
+        out_shape=jax.ShapeDtypeStruct(
+            (blocks * shard, low_width), jnp.bfloat16 if received is None else jnp.float32
+        ),
+        cost_estimate=pl.CostEstimate(
+            flops=4 * count * blocks * shard * low_width,
+            bytes_accessed=4 * count * blocks * shard,
+            transcendentals=0,
+        ),
+    )(where, *operands)
+
+
+def chunk_kernel(first, last, shard, where, *refs):
+    tok, gk, gl, down = refs[:4]
+    pieces, rest = refs[4:12], list(refs[12:])
+    acc = None if first else rest.pop(0)
+    low, up, live = (rest.pop(0) for _ in range(3)) if last else (None, None, None)
+    if not first:
+        rest.pop(0)
+    ig, out = rest[:2]
+    total = rest[2] if last else out
+    y, c, g = where[1], where[2], where[3]
+    half = shard // 2
+    for j, ref in enumerate(pieces):
+        yy = y if j < 4 else 1 - y
+        core = c if j % 4 < 2 else 1 - c
+        part = g if j % 2 == 0 else 1 - g
+        at = pl.ds(pl.multiple_of(2 * shard * yy + shard * core + half * part, half), half)
+        block = lax.dot_general(gk[...], ref[...], NT, preferred_element_type=jnp.float32)
+        block += lax.dot_general(gl[...], down[at, :], NT, preferred_element_type=jnp.float32)
+        ig[:, at] = block.astype(ig.dtype)
+        term = jnp.dot(tok[:, at], ref[...], preferred_element_type=jnp.float32)
+        if j == 0 and first:
+            total[...] = term
+        elif j == 0:
+            total[...] = acc[...] + term
+        else:
+            total[...] += term
+    if last:
+        done = total[...] + jnp.dot(low[...], up[...], preferred_element_type=jnp.float32)
+        out[...] = (done * live[...]).astype(out.dtype)
+
+
+def chunk(where, tokens, gk, gl, down, pieces, acc, ig, ending=()):
+    count, width = tokens.shape
+    features = gk.shape[1]
+    shard = 2 * pieces[0].shape[0]
+    depth = 4 * shard
+    first, last = acc is None, bool(ending)
+
+    def whole(a):
+        return pl.BlockSpec(a.shape, lambda i, w: (0, 0))
+
+    operands = [tokens, gk, gl, down, *pieces]
+    specs = [
+        pl.BlockSpec((count, depth), lambda i, w: (0, w[0])),
+        whole(gk),
+        whole(gl),
+        pl.BlockSpec((depth, down.shape[1]), lambda i, w: (w[0], 0)),
+        *[whole(p) for p in pieces],
+    ]
+    if not first:
+        operands.append(acc)
+        specs.append(whole(acc))
+    operands += ending
+    specs += [whole(e) for e in ending]
+    alias = {}
+    if not first:
+        alias = {len(operands) + 1: 0}
+        operands.append(ig)
+        specs.append(pl.BlockSpec(memory_space=pl.ANY))
+    return pl.pallas_call(
+        functools.partial(chunk_kernel, first, last, shard),
+        grid_spec=pltpu.PrefetchScalarGridSpec(
+            num_scalar_prefetch=1,
+            grid=(1,),
+            in_specs=specs,
+            out_specs=[
+                pl.BlockSpec((count, depth), lambda i, w: (0, w[0])),
+                pl.BlockSpec((count, features), lambda i, w: (0, 0)),
+            ],
+            scratch_shapes=[pltpu.VMEM((count, features), jnp.float32)] if last else [],
+        ),
+        out_shape=[
+            jax.ShapeDtypeStruct((count, width), jnp.bfloat16),
+            jax.ShapeDtypeStruct((count, features), jnp.bfloat16 if last else jnp.float32),
+        ],
+        input_output_aliases=alias,
+        compiler_params=pltpu.CompilerParams(vmem_limit_bytes=32 * 1024 * 1024),
+        cost_estimate=pl.CostEstimate(
+            flops=2 * count * depth * (2 * features + down.shape[1]),
+            bytes_accessed=2 * depth * features + 4 * count * (depth + features),
+            transcendentals=0,
+        ),
+    )(where, *operands)
+
+
+def plain_form(
     tokens, key_weight, adapter_down, adapter_up, key_cotangent, block_job, block_live, job_rank
 ):
     tok_count = tokens.shape[0]
@@ -78,6 +233,137 @@
     return (keys, input_grad, down_grad, up_grad)
 
 
+def per_device(
+    n, tokens, key_weight, adapter_down, adapter_up, key_cotangent, block_job, block_live, job_rank
+):
+    if n % 4 or key_weight.shape[0] % 256 or lax.axis_size("groups") != 2:
+        return plain_form(
+            tokens,
+            key_weight,
+            adapter_down,
+            adapter_up,
+            key_cotangent,
+            block_job,
+            block_live,
+            job_rank,
+        )
+    f32, bf16 = jnp.float32, jnp.bfloat16
+    outer = n // 4
+    count, width = tokens.shape
+    features = key_weight.shape[1]
+    shard = key_weight.shape[0]
+    jobs = job_rank.shape[0]
+    low_width = adapter_down.shape[1]
+    here = block_live.shape[0]
+    idx = lax.axis_index("fsdp")
+    g = lax.axis_index("groups")
+    z, y, c = idx // 4, (idx // 2) % 2, idx % 2
+
+    def swap(v, mask):
+        return lax.ppermute(v, "fsdp", [(s, s ^ mask) for s in range(n)])
+
+    def across(v):
+        return lax.ppermute(v, "groups", [(0, 1), (1, 0)])
+
+    def rows_of(v, i, size):
+        return lax.dynamic_slice_in_dim(v, i * size, size, 0)
+
+    local_job = rows_of(block_job, idx, here)
+    pair_job = rows_of(block_job, idx ^ 1, here)
+    position = jnp.arange(count, dtype=jnp.int32)
+    live = (position % BLOCK < jnp.repeat(block_live, BLOCK)).astype(f32)
+    columns = jnp.arange(low_width, dtype=jnp.int32)
+    col_job = columns // RANK
+    col_rank = jnp.repeat(job_rank, RANK)
+    col_scale = jnp.where(columns % RANK < col_rank, 16.0 / col_rank.astype(f32), 0.0)
+
+    def column_mask(job):
+        mine = col_job[None, :] == jnp.repeat(job, BLOCK)[:, None]
+        return mine.astype(f32) * col_scale[None, :]
+
+    colmask = column_mask(local_job) * live[:, None]
+    grad_keys = (key_cotangent.astype(f32) * live[:, None]).astype(bf16)
+
+    up_rows = adapter_up.shape[0]
+    tail = jnp.pad(block_live.astype(bf16), (0, 128 - here))
+    packed = jnp.concatenate(
+        [adapter_up, jnp.broadcast_to(tail[None, :], (up_rows, 128))], axis=1
+    )
+    gathered = jnp.concatenate(
+        [packed] + [swap(packed, 4 * k) for k in range(1, outer)], axis=0
+    )
+    gathered = jnp.concatenate([gathered, swap(gathered, 2)], axis=0)
+    gathered = jnp.concatenate([gathered, swap(gathered, 1)], axis=0)
+    at = jnp.arange(n * up_rows, dtype=jnp.int32)
+    place = at // up_rows
+    mask = 4 * (place % outer) + 2 * (place // outer % 2) + place // (2 * outer)
+    source = (idx ^ mask) * up_rows + at % up_rows
+    order = (at[:, None] == source[None, :]).astype(bf16)
+    ordered = jnp.dot(order, gathered, preferred_element_type=f32).astype(bf16)
+    up_full = ordered[:, :features]
+    live_all = ordered.reshape(n, up_rows, features + 128)[:, 0, features : features + here]
+    live_all = live_all.reshape(n * here).astype(f32)
+    onehot = (block_job[:, None] == jnp.arange(jobs, dtype=jnp.int32)[None, :]).astype(f32)
+    count_of = jnp.sum(onehot * live_all[:, None], axis=0)
+    norm = jnp.repeat(1.0 / jnp.sqrt(jnp.maximum(count_of, 1.0)), RANK)
+
+    down_full = lax.all_gather(adapter_down, "fsdp", axis=0, tiled=True)
+
+    places = 4 * jnp.arange(outer, dtype=jnp.int32)
+    far_at, near_at = places + 2 * (1 - y) + c, places + 2 * y + c
+    pair_keys = swap(grad_keys, 1)
+    pair_tokens = swap(
+        pick_columns(jnp.concatenate([far_at, near_at]) + 1 - 2 * c, tokens, shard), 1
+    )
+
+    def grad_low_of(keys, mask):
+        return (
+            lax.dot_general(keys, up_full, NT, preferred_element_type=f32) * mask
+        ).astype(bf16)
+
+    grad_low = grad_low_of(grad_keys, colmask)
+    pair_low = grad_low_of(pair_keys, column_mask(pair_job))
+    far = part_sums(far_at, 0, tokens, pair_tokens, grad_low, pair_low, shard)
+    near = part_sums(
+        near_at, outer, tokens, pair_tokens, grad_low, pair_low, shard, swap(far, 2)
+    )
+    owned = rows_of(near, z, shard)
+    for k in range(1, outer):
+        owned = owned + swap(rows_of(near, z ^ k, shard).astype(bf16), 4 * k).astype(f32)
+    down_grad = owned * norm[None, :]
+
+    low = (jnp.dot(tokens, down_full, preferred_element_type=f32) * colmask).astype(bf16)
+    up_term = lax.dot_general(low, grad_keys, TN, preferred_element_type=f32)
+    up_term = up_term.reshape(outer, 2, 2, up_rows, features)
+    up_sum = lax.dynamic_index_in_dim(up_term, c, 2, False) + swap(
+        lax.dynamic_index_in_dim(up_term, 1 - c, 2, False), 1
+    )
+    up_sum = lax.dynamic_index_in_dim(up_sum, y, 1, False) + swap(
+        lax.dynamic_index_in_dim(up_sum, 1 - y, 1, False), 2
+    )
+    up_owned = lax.dynamic_index_in_dim(up_sum, z, 0, False)
+    for k in range(1, outer):
+        up_owned = up_owned + swap(lax.dynamic_index_in_dim(up_sum, z ^ k, 0, False), 4 * k)
+    up_grad = up_owned * rows_of(norm, idx, up_rows)[:, None]
+
+    half = shard // 2
+    mine, rest = rows_of(key_weight, g, half), rows_of(key_weight, 1 - g, half)
+    acc = ig = None
+    for k in range(outer):
+        near_half = mine if k == 0 else swap(mine, 4 * k)
+        far_half = swap(near_half, 2)
+        near_rest = rest if k == 0 else across(near_half)
+        pieces = [near_half, near_rest, swap(near_half, 1), swap(near_rest, 1)]
+        far_rest = across(far_half)
+        pieces += [far_half, far_rest, swap(far_half, 1), swap(far_rest, 1)]
+        where = jnp.stack([z ^ k, y, c, g]).astype(jnp.int32)
+        ending = [low, up_full, live[:, None]] if k == outer - 1 else []
+        ig, acc = chunk(
+            where, tokens, grad_keys, grad_low, down_full, pieces, acc, ig, ending
+        )
+    return (acc, ig, down_grad, up_grad)
+
+
 def solution(mesh):
     placed = (
         P(("groups", "fsdp"), None),
@@ -90,14 +376,9 @@
         P("groups"),
     )
     return jax.shard_map(
-        per_device,
+        functools.partial(per_device, mesh.shape["fsdp"]),
         mesh=mesh,
         in_specs=placed,
-        out_specs=(
-            P(("groups", "fsdp"), None),
-            P(("groups", "fsdp"), None),
-            P(("groups", "fsdp"), None),
-            P(("groups", "fsdp"), None),
-        ),
+        out_specs=(P(("groups", "fsdp"), None),) * 4,
         check_vma=False,
     )

time: 347 us -> 216 us (0.62)
  blocking collectives: 162 us -> 0 us
  starting transfers between devices: 4.81 us -> 48.5 us
  matrix products: 47.3 us -> 7.45 us
  Pallas kernels: 0 us -> 39.8 us
  waiting for transfers between devices: 99.9 us -> 75.2 us
  other arithmetic: 2.5 us -> 10.4 us
    psum x1 -> x0, blocking collectives: 103 us -> none  [per_device(): count = lax.psum(local_count, 'fsdp')]
    all_gather x2 -> x1, waiting for transfers between devices: 98.5 us -> 0.01 us  [per_device(): down_full = lax.all_gather(adapter_down, 'fsdp', axis=0, tiled=True)]
    ppermute x0 -> x46, waiting for transfers between devices: none -> 74.5 us  [the longest x39 63.8 us: swap(): return lax.ppermute(v, 'fsdp', [(s, s ^ mask) for s in range(n)])]
    all_gather x2 -> x0, blocking collectives: 59.1 us -> none  [the longest x1 35.1 us: per_device(): up_full = lax.all_gather(adapter_up, 'fsdp', axis=0, tiled=True)]
    ppermute x0 -> x46, starting transfers between devices: none -> 48.4 us  [the longest x39 40.8 us: swap(): return lax.ppermute(v, 'fsdp', [(s, s ^ mask) for s in range(n)])]
    dot_general x11 -> x5, matrix products: 47.3 us -> 7.45 us  [the longest x1 4.8 us: per_device(): jnp.dot(tokens, down_full, preferred_element_type=f32) * colmask]
    pallas_call x0 -> x7, Pallas kernels: none -> 39.8 us  [the longest x4 22.9 us: chunk(): pl.pallas_call(functools.partial(chunk_kernel, first, last, shard), grid_...]
    all_to_all x1 -> x0, local copies, waits for them, and re-layouts: 6.42 us -> none  [per_device(): lax.all_to_all(tokens, 'fsdp', split_axis=1, concat_axis=0, tiled=True)]
  transfers between devices with their start and end apart: 4 -> 47, of which waited for: 2 -> 9; matrix products, arithmetic and copies ran while one was open for 7% -> 14% of each run, Pallas kernels for 0% -> 19%
where the time goes in v1:
time: 216 us; the launch traced here: 215 us
  waiting for transfers between devices  75.2 us (35%)
  starting transfers between devices  48.5 us (22%)
  Pallas kernels  39.8 us (18%)
  local copies, waits for them, and re-layouts  18.8 us (9%)
  between operations  14.4 us (7%)
  other arithmetic  10.4 us (5%)
  matrix products  7.45 us (3%)
    ppermute x39, waiting for transfers between devices, swap(): return lax.ppermute(v, 'fsdp', [(s, s ^ mask) for s in range(n)])  63.8 us
    ppermute x39, starting transfers between devices, swap(): return lax.ppermute(v, 'fsdp', [(s, s ^ mask) for s in range(n)])  40.8 us
    pallas_call x4, Pallas kernels, chunk(): pl.pallas_call(functools.partial(chunk_kernel, first, last, shard), grid_...  22.9 us
    ppermute x7, waiting for transfers between devices, across(): return lax.ppermute(v, 'groups', [(0, 1), (1, 0)])  10.7 us
    pallas_call x2, Pallas kernels, part_sums(): pl.pallas_call(part_kernel, grid_spec=pltpu.PrefetchScalarGridSpec(num_sc...  10.5 us
    unnamed x47, local copies, waits for them, and re-layouts  8.16 us
    ppermute x7, starting transfers between devices, across(): return lax.ppermute(v, 'groups', [(0, 1), (1, 0)])  7.64 us
    pallas_call x1, Pallas kernels, pick_columns(): pl.pallas_call(pick_kernel, grid_spec=pltpu.PrefetchScalarGridSpec(num_sc...  6.32 us
  transfers between devices with their start and end apart: 47, of which 9 were waited for; matrix products, arithmetic and copies ran while one was open for 14% of the time, Pallas kernels for 19%

profile of v1, /device:TPU:0, one launch (start us, length us, event | category | flops | bytes accessed | tf_op | source)
XLA Modules:
  0.0 214.6 jit_solution(14185390144260591269)
XLA Ops:
  10.0 3.0 %collective-permute-start = (bf16[16,1152]{1,0:T(8,128)(2,1)S(1)}, bf16[16,1152]{1,0:T(8,128)(2,1)S(1)}, u32[]{:S(2)}, u32[]{:S(2)}) collective-permute-start(bf16[16,1152]{1,0:T(8,128)(2,1)S(1)} %get-tuple-element.38), channel_id=1, source_target_pairs={{0,4},{1,5},{2,6},{3,7},{4,0},{5,1},{6,2},{7,3},{8,12},{9,13},{10,... | collective-permute-start | bytes 110600 | tf_op jit(solution)/shard_map/ppermute | solution.py:263
  13.0 2.6 %collective-permute-start.1 = (bf16[16,1152]{1,0:T(8,128)(2,1)S(1)}, bf16[16,1152]{1,0:T(8,128)(2,1)S(1)}, u32[]{:S(2)}, u32[]{:S(2)}) collective-permute-start(bf16[16,1152]{1,0:T(8,128)(2,1)S(1)} %get-tuple-element.38), channel_id=1, source_target_pairs={{0,8},{1,9},{2,10},{3,11},{4,12},{5,13},{6,14},{7,15},{8,0},{9,1},... | collective-permute-start | bytes 110600 | tf_op jit(solution)/shard_map/ppermute | solution.py:263
  23.0 6.3 %shard_map.115 = bf16[256,4096]{1,0:T(8,128)(2,1)} custom-call(s32[8]{0:T(128)} %fusion.18.where, bf16[256,8192]{1,0:T(8,128)(2,1)} %mine.3), custom_call_target="tpu_custom_call" | custom-call | bytes 4194304 | tf_op jit(solution)/shard_map/pallas_call | solution.py:25
  32.2 4.0 %collective-permute-done.3 = bf16[64,1152]{1,0:T(8,128)(2,1)S(1)} collective-permute-done((bf16[64,1152]{1,0:T(8,128)(2,1)S(1)}, bf16[64,1152]{1,0:T(8,128)(2,1)S(1)}, u32[]{:S(2)}, u32[]{:S(2)}) %collective-permute-start.3) | collective-permute-done | bytes 147488 | tf_op jit(solution)/shard_map/ppermute | solution.py:263
  41.2 5.1 %shard_map.116 = bf16[2048,256]{1,0:T(8,128)(2,1)} custom-call(s32[4]{0:T(128)} %copy-done.19, bf16[256,8192]{1,0:T(8,128)(2,1)} %mine.3, bf16[256,4096]{1,0:T(8,128)(2,1)} %collective-permute-done.35.theirs, bf16[256,256]{1,0:T(8,128)(2,1)} %fusion.1.refs_2_.low_mine, bf16[256,256]{1,0:T(8,128)(2,1)} %fusion.2.low_theirs), custom_call_target="tpu_custom_call" | custom-call | flops 536870912 | bytes 2097152 | tf_op jit(solution)/shard_map/pallas_call | solution.py:64
  48.3 3.5 %collective-permute-start.13 = (bf16[256,1024]{1,0:T(8,128)(2,1)S(1)}, bf16[256,1024]{1,0:T(8,128)(2,1)}, u32[]{:S(2)}, u32[]{:S(2)}) collective-permute-start(bf16[256,1024]{1,0:T(8,128)(2,1)S(1)} %get-tuple-element.24.refs_4_), channel_id=1, source_target_pairs={{0,8},{1,9},{2,10},{3,11},{4,12},{5,13},{6,14},{7,15},{8,0},{9,1},... | collective-permute-start | bytes 1572872 | tf_op jit(solution)/shard_map/ppermute | solution.py:263
  54.1 29.5 %collective-permute-done.21.refs_4_ = bf16[256,1024]{1,0:T(8,128)(2,1)} collective-permute-done((bf16[256,1024]{1,0:T(8,128)(2,1)S(1)}, bf16[256,1024]{1,0:T(8,128)(2,1)}, u32[]{:S(2)}, u32[]{:S(2)}) %collective-permute-start.21) | collective-permute-done | bytes 524320 | tf_op jit(solution)/shard_map/ppermute | solution.py:263
  85.1 11.5 %collective-permute-done.5.refs_4_ = bf16[256,1024]{1,0:T(8,128)(2,1)S(1)} collective-permute-done((bf16[256,1024]{1,0:T(8,128)(2,1)S(1)}, bf16[256,1024]{1,0:T(8,128)(2,1)S(1)}, u32[]{:S(2)}, u32[]{:S(2)}) %collective-permute-start.5) | collective-permute-done | bytes 524320 | tf_op jit(solution)/shard_map/ppermute | solution.py:263
  102.3 5.4 %shard_map.117 = f32[2048,256]{1,0:T(8,128)} custom-call(s32[4]{0:T(128)} %copy-done.18, bf16[256,8192]{1,0:T(8,128)(2,1)} %mine.3, bf16[256,4096]{1,0:T(8,128)(2,1)} %collective-permute-done.35.theirs, bf16[256,256]{1,0:T(8,128)(2,1)} %fusion.1.refs_2_.low_mine, bf16[256,256]{1,0:T(8,128)(2,1)} %fusion.2.low_theirs, ...), custom_call_target="tpu_custom_call" | custom-call | flops 536870912 | bytes 2097152 | tf_op jit(solution)/shard_map/pallas_call | solution.py:64
  107.7 2.3 %dynamic-slice_convert_fusion.2 = (bf16[512,256]{1,0:T(8,128)(2,1)}, bf16[512,256]{1,0:T(8,128)(2,1)}, bf16[512,256]{1,0:T(8,128)(2,1)}) fusion(f32[2048,256]{1,0:T(8,128)} %shard_map.117, s32[]{:T(128)S(6)} %select_n.180, s32[]{:T(128)S(6)} %select_n.182, s32[]{:T(128)S(6)} %select_n.181), kind=kLoop, calls=%fused_computation.13 | loop fusion | bytes 1572876 | tf_op jit(solution)/shard_map/convert_element_type | solution.py:332
  113.7 4.8 %fusion.refs_13_ = bf16[256,256]{1,0:T(8,128)(2,1)S(1)} fusion(bf16[256,8192]{1,0:T(8,128)(2,1)} %mine.3, bf16[8192,256]{1,0:T(8,128)(2,1)} %all-gather.2.cloned.1.call-done.refs_3_, f32[256]{0:T(256)S(1)} %compare_convert_fusion, f32[256]{0:T(256)S(1)} %compare_select_fusion.2, s32[256]{0:T(256)S(1)} %and_select_fusion.2, s32[256]{0:T(256)S(1)} %broadcast_bitcast_fusion.1), kind=kOutput, calls=%fused_computation.4 | convolution fusion | flops 1074069504 | bytes 8523776 | tf_op jit(solution)/shard_map/dot_general | solution.py:335
  118.5 6.5 %collective-permute-done.14.refs_5_ = bf16[256,1024]{1,0:T(8,128)(2,1)} collective-permute-done((bf16[256,1024]{1,0:T(8,128)(2,1)}, bf16[256,1024]{1,0:T(8,128)(2,1)}, u32[]{:S(2)}, u32[]{:S(2)}) %collective-permute-start.14) | collective-permute-done | bytes 524320 | tf_op jit(solution)/shard_map/ppermute | solution.py:266
  125.0 10.8 %collective-permute-start.38 = (bf16[512,256]{1,0:T(8,128)(2,1)S(1)}, bf16[512,256]{1,0:T(8,128)(2,1)S(1)}, u32[]{:S(2)}, u32[]{:S(2)}) collective-permute-start(bf16[512,256]{1,0:T(8,128)(2,1)S(1)} %copy-done.13), channel_id=1, source_target_pairs={{0,4},{1,5},{2,6},{3,7},{4,0},{5,1},{6,2},{7,3},{8,12},{9,13},{10,... | collective-permute-start | bytes 786440 | tf_op jit(solution)/shard_map/ppermute | solution.py:263
  135.9 2.4 %collective-permute-start.40 = (bf16[512,256]{1,0:T(8,128)(2,1)S(1)}, bf16[512,256]{1,0:T(8,128)(2,1)S(1)}, u32[]{:S(2)}, u32[]{:S(2)}) collective-permute-start(bf16[512,256]{1,0:T(8,128)(2,1)S(1)} %copy-done.11), channel_id=1, source_target_pairs={{0,12},{1,13},{2,14},{3,15},{4,8},{5,9},{6,10},{7,11},{8,4},{9,5},... | collective-permute-start | bytes 786440 | tf_op jit(solution)/shard_map/ppermute | solution.py:263
  140.1 4.8 %collective-permute-done.38 = bf16[512,256]{1,0:T(8,128)(2,1)S(1)} collective-permute-done((bf16[512,256]{1,0:T(8,128)(2,1)S(1)}, bf16[512,256]{1,0:T(8,128)(2,1)S(1)}, u32[]{:S(2)}, u32[]{:S(2)}) %collective-permute-start.38) | collective-permute-done | bytes 262176 | tf_op jit(solution)/shard_map/ppermute | solution.py:263
  144.9 12.1 %collective-permute-done.39 = bf16[512,256]{1,0:T(8,128)(2,1)S(1)} collective-permute-done((bf16[512,256]{1,0:T(8,128)(2,1)S(1)}, bf16[512,256]{1,0:T(8,128)(2,1)S(1)}, u32[]{:S(2)}, u32[]{:S(2)}) %collective-permute-start.39) | collective-permute-done | bytes 262176 | tf_op jit(solution)/shard_map/ppermute | solution.py:263
  161.0 2.3 %add_multiply_fusion = f32[512,256]{1,0:T(8,128)} fusion(bf16[512,256]{1,0:T(8,128)(2,1)} %copy-done.16, bf16[512,256]{1,0:T(8,128)(2,1)} %copy-done.15, bf16[512,256]{1,0:T(8,128)(2,1)} %copy-done.14, f32[2048,256]{1,0:T(8,128)} %shard_map.117, s32[]{:T(128)S(6)} %select_n.179, f32[256]{0:T(256)} %mul.157), kind=kLoop, calls=%fused_computation.10 | loop fusion | flops 917504 | bytes 1836036 | tf_op jit(solution)/shard_map/mul | solution.py:333
  169.1 5.5 %shard_map.111 = (bf16[256,8192]{1,0:T(8,128)(2,1)}, f32[256,1024]{1,0:T(8,128)S(1)}) custom-call(s32[4]{0:T(128)S(1)} %add_add_fusion.3.where, bf16[256,8192]{1,0:T(8,128)(2,1)S(1)} %copy-done, bf16[256,1024]{1,0:T(8,128)(2,1)S(1)} %multiply_convert_fusion.refs_1_, bf16[256,256]{1,0:T(8,128)(2,1)S(1)} %copy-done.2, bf16[8192,256]{1,0:T(8,128)(2,1)S(1)} %copy-done.1, ...), custom_call_target="tpu_custom_call" | custom-call | flops 2415919104 | bytes 7340032 | tf_op jit(solution)/shard_map/pallas_call | solution.py:139
  178.4 6.1 %shard_map.112 = (bf16[256,8192]{1,0:T(8,128)(2,1)}, f32[256,1024]{1,0:T(8,128)S(1)}) custom-call(s32[4]{0:T(128)S(1)} %add_add_fusion.2.where, bf16[256,8192]{1,0:T(8,128)(2,1)S(1)} %copy-done, bf16[256,1024]{1,0:T(8,128)(2,1)S(1)} %multiply_convert_fusion.refs_1_, bf16[256,256]{1,0:T(8,128)(2,1)S(1)} %copy-done.2, ...), custom_call_target="tpu_custom_call", output_to_operand_aliasing={{0}: (14, {})} | custom-call | flops 2415919104 | bytes 7340032 | tf_op jit(solution)/shard_map/pallas_call | solution.py:139
  185.1 4.1 %collective-permute-done.10.refs_9_ = bf16[256,1024]{1,0:T(8,128)(2,1)S(1)} collective-permute-done((bf16[256,1024]{1,0:T(8,128)(2,1)}, bf16[256,1024]{1,0:T(8,128)(2,1)S(1)}, u32[]{:S(2)}, u32[]{:S(2)}) %collective-permute-start.10) | collective-permute-done | bytes 524320 | tf_op jit(solution)/shard_map/ppermute | solution.py:266
  189.7 5.8 %shard_map.113 = (bf16[256,8192]{1,0:T(8,128)(2,1)}, f32[256,1024]{1,0:T(8,128)S(1)}) custom-call(s32[4]{0:T(128)S(1)} %add_add_fusion.1.where, bf16[256,8192]{1,0:T(8,128)(2,1)S(1)} %copy-done, bf16[256,1024]{1,0:T(8,128)(2,1)S(1)} %multiply_convert_fusion.refs_1_, bf16[256,256]{1,0:T(8,128)(2,1)S(1)} %copy-done.2, ...), custom_call_target="tpu_custom_call", output_to_operand_aliasing={{0}: (14, {})} | custom-call | flops 2415919104 | bytes 7340032 | tf_op jit(solution)/shard_map/pallas_call | solution.py:139
  195.6 3.4 %collective-permute-start.43 = (f32[16,1024]{1,0:T(8,128)S(1)}, f32[16,1024]{1,0:T(8,128)S(1)}, u32[]{:S(2)}, u32[]{:S(2)}) collective-permute-start(f32[16,1024]{1,0:T(8,128)S(1)} %get-tuple-element.25), channel_id=1, source_target_pairs={{0,4},{1,5},{2,6},{3,7},{4,0},{5,1},{6,2},{7,3},{8,12},{9,13},{10,... | collective-permute-start | bytes 196616 | tf_op jit(solution)/shard_map/ppermute | solution.py:263
  199.0 2.4 %collective-permute-start.45 = (f32[16,1024]{1,0:T(8,128)S(1)}, f32[16,1024]{1,0:T(8,128)S(1)}, u32[]{:S(2)}, u32[]{:S(2)}) collective-permute-start(f32[16,1024]{1,0:T(8,128)S(1)} %get-tuple-element.26), channel_id=1, source_target_pairs={{0,12},{1,13},{2,14},{3,15},{4,8},{5,9},{6,10},{7,11},{8,4},{9,5},... | collective-permute-start | bytes 196616 | tf_op jit(solution)/shard_map/ppermute | solution.py:263
  201.4 5.6 %shard_map.114 = (bf16[256,8192]{1,0:T(8,128)(2,1)}, bf16[256,1024]{1,0:T(8,128)(2,1)}) custom-call(s32[4]{0:T(128)S(1)} %add_add_fusion.where, bf16[256,8192]{1,0:T(8,128)(2,1)S(1)} %copy-done, bf16[256,1024]{1,0:T(8,128)(2,1)S(1)} %multiply_convert_fusion.refs_1_, bf16[256,256]{1,0:T(8,128)(2,1)S(1)} %copy-done.2, ...), custom_call_target="tpu_custom_call", output_to_operand_aliasing={{0}: (17, {})} | custom-call | flops 2415919104 | bytes 7340032 | tf_op jit(solution)/shard_map/pallas_call | solution.py:139
  (176 shorter events, 50.3 us)
Async XLA Ops:
  7.2 106.5 %all-gather.2.cloned.1.call-start = ((), (), s32[]{:S(2)}) async-start(), calls=%async_computation | async-start | bytes 4456448 | tf_op jit(solution)/shard_map/all_gather | solution.py:310
  10.0 19.4 %collective-permute-start = (bf16[16,1152]{1,0:T(8,128)(2,1)S(1)}, bf16[16,1152]{1,0:T(8,128)(2,1)S(1)}, u32[]{:S(2)}, u32[]{:S(2)}) collective-permute-start(bf16[16,1152]{1,0:T(8,128)(2,1)S(1)} %get-tuple-element.38), channel_id=1, source_target_pairs={{0,4},{1,5},{2,6},{3,7},{4,0},{5,1},{6,2},{7,3},{8,12},{9,13},{10,... | collective-permute-start | bytes 110600 | tf_op jit(solution)/shard_map/ppermute | solution.py:263
  16.9 31.4 %collective-permute-start.31 = (bf16[256,1024]{1,0:T(8,128)(2,1)S(1)}, bf16[256,1024]{1,0:T(8,128)(2,1)S(1)}, u32[]{:S(2)}, u32[]{:S(2)}) collective-permute-start(bf16[256,1024]{1,0:T(8,128)(2,1)S(1)} %get-tuple-element.24.refs_4_), channel_id=1, source_target_pairs={{0,2},{1,3},{2,0},{3,1},{4,6},{5,7},{6,4},{7,5},{8,10},{9,11},{10,... | collective-permute-start | bytes 1572872 | tf_op jit(solution)/shard_map/ppermute | solution.py:263
  18.7 33.2 %collective-permute-start.29 = (bf16[256,1024]{1,0:T(8,128)(2,1)S(1)}, bf16[256,1024]{1,0:T(8,128)(2,1)S(1)}, u32[]{:S(2)}, u32[]{:S(2)}) collective-permute-start(bf16[256,1024]{1,0:T(8,128)(2,1)S(1)} %get-tuple-element.24.refs_4_), channel_id=1, source_target_pairs={{0,1},{1,0},{2,3},{3,2},{4,5},{5,4},{6,7},{7,6},{8,9},{9,8},{10,11... | collective-permute-start | bytes 1572872 | tf_op jit(solution)/shard_map/ppermute | solution.py:263
  46.3 52.6 %collective-permute-start.37 = (bf16[2048,256]{1,0:T(8,128)(2,1)}, bf16[2048,256]{1,0:T(8,128)(2,1)}, u32[]{:S(2)}, u32[]{:S(2)}) collective-permute-start(bf16[2048,256]{1,0:T(8,128)(2,1)} %shard_map.116), channel_id=1, source_target_pairs={{0,2},{1,3},{2,0},{3,1},{4,6},{5,7},{6,4},{7,5},{8,10},{9,11},{10,... | collective-permute-start | bytes 3145736 | tf_op jit(solution)/shard_map/ppermute | solution.py:263
  47.9 35.7 %collective-permute-start.21 = (bf16[256,1024]{1,0:T(8,128)(2,1)S(1)}, bf16[256,1024]{1,0:T(8,128)(2,1)}, u32[]{:S(2)}, u32[]{:S(2)}) collective-permute-start(bf16[256,1024]{1,0:T(8,128)(2,1)S(1)} %get-tuple-element.24.refs_4_), channel_id=1, source_target_pairs={{0,4},{1,5},{2,6},{3,7},{4,0},{5,1},{6,2},{7,3},{8,12},{9,13},{10,... | collective-permute-start | bytes 1572872 | tf_op jit(solution)/shard_map/ppermute | solution.py:263
  48.3 35.3 %collective-permute-start.13 = (bf16[256,1024]{1,0:T(8,128)(2,1)S(1)}, bf16[256,1024]{1,0:T(8,128)(2,1)}, u32[]{:S(2)}, u32[]{:S(2)}) collective-permute-start(bf16[256,1024]{1,0:T(8,128)(2,1)S(1)} %get-tuple-element.24.refs_4_), channel_id=1, source_target_pairs={{0,8},{1,9},{2,10},{3,11},{4,12},{5,13},{6,14},{7,15},{8,0},{9,1},... | collective-permute-start | bytes 1572872 | tf_op jit(solution)/shard_map/ppermute | solution.py:263
  51.8 44.8 %collective-permute-start.5 = (bf16[256,1024]{1,0:T(8,128)(2,1)S(1)}, bf16[256,1024]{1,0:T(8,128)(2,1)S(1)}, u32[]{:S(2)}, u32[]{:S(2)}) collective-permute-start(bf16[256,1024]{1,0:T(8,128)(2,1)S(1)} %get-tuple-element.24.refs_4_), channel_id=1, source_target_pairs={{0,12},{1,13},{2,14},{3,15},{4,8},{5,9},{6,10},{7,11},{8,4},{9,5},... | collective-permute-start | bytes 1572872 | tf_op jit(solution)/shard_map/ppermute | solution.py:263
  52.3 45.8 %collective-permute-start.32 = (bf16[256,1024]{1,0:T(8,128)(2,1)S(1)}, bf16[256,1024]{1,0:T(8,128)(2,1)S(1)}, u32[]{:S(2)}, u32[]{:S(2)}) collective-permute-start(bf16[256,1024]{1,0:T(8,128)(2,1)S(1)} %collective-permute-done.31.refs_8_), channel_id=1, source_target_pairs={{0,16},{16,0},{1,17},{17,1},{2,18},{18,2},{3,19},{19,3},{4,20},{20... | collective-permute-start | bytes 1572872 | tf_op jit(solution)/shard_map/ppermute | solution.py:266
  83.6 26.4 %collective-permute-start.33 = (bf16[256,1024]{1,0:T(8,128)(2,1)S(1)}, bf16[256,1024]{1,0:T(8,128)(2,1)}, u32[]{:S(2)}, u32[]{:S(2)}) collective-permute-start(bf16[256,1024]{1,0:T(8,128)(2,1)S(1)} %collective-permute-done.31.refs_8_), channel_id=1, source_target_pairs={{0,1},{1,0},{2,3},{3,2},{4,5},{5,4},{6,7},{7,6},{8,9},{9,8},{10,11... | collective-permute-start | bytes 1572872 | tf_op jit(solution)/shard_map/ppermute | solution.py:263
  83.6 26.9 %collective-permute-start.25 = (bf16[256,1024]{1,0:T(8,128)(2,1)}, bf16[256,1024]{1,0:T(8,128)(2,1)}, u32[]{:S(2)}, u32[]{:S(2)}) collective-permute-start(bf16[256,1024]{1,0:T(8,128)(2,1)} %collective-permute-done.21.refs_4_), channel_id=1, source_target_pairs={{0,2},{1,3},{2,0},{3,1},{4,6},{5,7},{6,4},{7,5},{8,10},{9,11},{10,... | collective-permute-start | bytes 1572872 | tf_op jit(solution)/shard_map/ppermute | solution.py:263
  110.5 25.3 %collective-permute-start.15 = (bf16[256,1024]{1,0:T(8,128)(2,1)}, bf16[256,1024]{1,0:T(8,128)(2,1)}, u32[]{:S(2)}, u32[]{:S(2)}) collective-permute-start(bf16[256,1024]{1,0:T(8,128)(2,1)} %collective-permute-done.13.refs_4_), channel_id=1, source_target_pairs={{0,1},{1,0},{2,3},{3,2},{4,5},{5,4},{6,7},{7,6},{8,9},{9,8},{10,11... | collective-permute-start | bytes 1572872 | tf_op jit(solution)/shard_map/ppermute | solution.py:263
  110.6 25.2 %collective-permute-start.9 = (bf16[256,1024]{1,0:T(8,128)(2,1)S(1)}, bf16[256,1024]{1,0:T(8,128)(2,1)}, u32[]{:S(2)}, u32[]{:S(2)}) collective-permute-start(bf16[256,1024]{1,0:T(8,128)(2,1)S(1)} %collective-permute-done.5.refs_4_), channel_id=1, source_target_pairs={{0,2},{1,3},{2,0},{3,1},{4,6},{5,7},{6,4},{7,5},{8,10},{9,11},{10,... | collective-permute-start | bytes 1572872 | tf_op jit(solution)/shard_map/ppermute | solution.py:263
  112.2 26.5 %collective-permute-start.6 = (bf16[256,1024]{1,0:T(8,128)(2,1)S(1)}, bf16[256,1024]{1,0:T(8,128)(2,1)}, u32[]{:S(2)}, u32[]{:S(2)}) collective-permute-start(bf16[256,1024]{1,0:T(8,128)(2,1)S(1)} %collective-permute-done.5.refs_4_), channel_id=1, source_target_pairs={{0,16},{16,0},{1,17},{17,1},{2,18},{18,2},{3,19},{19,3},{4,20},{20... | collective-permute-start | bytes 1572872 | tf_op jit(solution)/shard_map/ppermute | solution.py:266
  113.6 26.5 %collective-permute-start.34 = (bf16[256,1024]{1,0:T(8,128)(2,1)}, bf16[256,1024]{1,0:T(8,128)(2,1)}, u32[]{:S(2)}, u32[]{:S(2)}) collective-permute-start(bf16[256,1024]{1,0:T(8,128)(2,1)} %copy-done.5), channel_id=1, source_target_pairs={{0,1},{1,0},{2,3},{3,2},{4,5},{5,4},{6,7},{7,6},{8,9},{9,8},{10,11... | collective-permute-start | bytes 1572872 | tf_op jit(solution)/shard_map/ppermute | solution.py:263
  125.0 19.8 %collective-permute-start.38 = (bf16[512,256]{1,0:T(8,128)(2,1)S(1)}, bf16[512,256]{1,0:T(8,128)(2,1)S(1)}, u32[]{:S(2)}, u32[]{:S(2)}) collective-permute-start(bf16[512,256]{1,0:T(8,128)(2,1)S(1)} %copy-done.13), channel_id=1, source_target_pairs={{0,4},{1,5},{2,6},{3,7},{4,0},{5,1},{6,2},{7,3},{8,12},{9,13},{10,... | collective-permute-start | bytes 786440 | tf_op jit(solution)/shard_map/ppermute | solution.py:263
  135.8 21.1 %collective-permute-start.39 = (bf16[512,256]{1,0:T(8,128)(2,1)S(1)}, bf16[512,256]{1,0:T(8,128)(2,1)S(1)}, u32[]{:S(2)}, u32[]{:S(2)}) collective-permute-start(bf16[512,256]{1,0:T(8,128)(2,1)S(1)} %copy-done.12), channel_id=1, source_target_pairs={{0,8},{1,9},{2,10},{3,11},{4,12},{5,13},{6,14},{7,15},{8,0},{9,1},... | collective-permute-start | bytes 786440 | tf_op jit(solution)/shard_map/ppermute | solution.py:263
  135.9 21.7 %collective-permute-start.40 = (bf16[512,256]{1,0:T(8,128)(2,1)S(1)}, bf16[512,256]{1,0:T(8,128)(2,1)S(1)}, u32[]{:S(2)}, u32[]{:S(2)}) collective-permute-start(bf16[512,256]{1,0:T(8,128)(2,1)S(1)} %copy-done.11), channel_id=1, source_target_pairs={{0,12},{1,13},{2,14},{3,15},{4,8},{5,9},{6,10},{7,11},{8,4},{9,5},... | collective-permute-start | bytes 786440 | tf_op jit(solution)/shard_map/ppermute | solution.py:263
  138.6 24.6 %collective-permute-start.26 = (bf16[256,1024]{1,0:T(8,128)(2,1)}, bf16[256,1024]{1,0:T(8,128)(2,1)}, u32[]{:S(2)}, u32[]{:S(2)}) collective-permute-start(bf16[256,1024]{1,0:T(8,128)(2,1)} %collective-permute-done.25.refs_8_), channel_id=1, source_target_pairs={{0,16},{16,0},{1,17},{17,1},{2,18},{18,2},{3,19},{19,3},{4,20},{20... | collective-permute-start | bytes 1572872 | tf_op jit(solution)/shard_map/ppermute | solution.py:266
  140.1 34.5 %collective-permute-start.27 = (bf16[256,1024]{1,0:T(8,128)(2,1)}, bf16[256,1024]{1,0:T(8,128)(2,1)}, u32[]{:S(2)}, u32[]{:S(2)}) collective-permute-start(bf16[256,1024]{1,0:T(8,128)(2,1)} %collective-permute-done.25.refs_8_), channel_id=1, source_target_pairs={{0,1},{1,0},{2,3},{3,2},{4,5},{5,4},{6,7},{7,6},{8,9},{9,8},{10,11... | collective-permute-start | bytes 1572872 | tf_op jit(solution)/shard_map/ppermute | solution.py:263
  144.9 29.8 %collective-permute-start.24 = (bf16[256,1024]{1,0:T(8,128)(2,1)}, bf16[256,1024]{1,0:T(8,128)(2,1)}, u32[]{:S(2)}, u32[]{:S(2)}) collective-permute-start(bf16[256,1024]{1,0:T(8,128)(2,1)} %collective-permute-done.22.refs_5_), channel_id=1, source_target_pairs={{0,1},{1,0},{2,3},{3,2},{4,5},{5,4},{6,7},{7,6},{8,9},{9,8},{10,11... | collective-permute-start | bytes 1572872 | tf_op jit(solution)/shard_map/ppermute | solution.py:263
  157.0 18.1 %collective-permute-start.18 = (bf16[256,1024]{1,0:T(8,128)(2,1)}, bf16[256,1024]{1,0:T(8,128)(2,1)}, u32[]{:S(2)}, u32[]{:S(2)}) collective-permute-start(bf16[256,1024]{1,0:T(8,128)(2,1)} %collective-permute-done.17.refs_8_), channel_id=1, source_target_pairs={{0,16},{16,0},{1,17},{17,1},{2,18},{18,2},{3,19},{19,3},{4,20},{20... | collective-permute-start | bytes 1572872 | tf_op jit(solution)/shard_map/ppermute | solution.py:266
  157.5 19.0 %collective-permute-start.41 = (f32[4,2,16,1024]{3,2,1,0:T(8,128)}, f32[4,2,16,1024]{3,2,1,0:T(8,128)}, u32[]{:S(2)}, u32[]{:S(2)}) collective-permute-start(f32[4,2,16,1024]{3,2,1,0:T(8,128)} %dynamic-slice_bitcast_fusion), channel_id=1, source_target_pairs={{0,1},{1,0},{2,3},{3,2},{4,5},{5,4},{6,7},{7,6},{8,9},{9,8},{10,11... | collective-permute-start | bytes 1572872 | tf_op jit(solution)/shard_map/ppermute | solution.py:263
  177.7 17.7 %collective-permute-start.42 = (f32[4,16,1024]{2,1,0:T(8,128)S(1)}, f32[4,16,1024]{2,1,0:T(8,128)S(1)}, u32[]{:S(2)}, u32[]{:S(2)}) collective-permute-start(f32[4,16,1024]{2,1,0:T(8,128)S(1)} %dynamic-slice_bitcast_fusion.1), channel_id=1, source_target_pairs={{0,2},{1,3},{2,0},{3,1},{4,6},{5,7},{6,4},{7,5},{8,10},{9,11},{10,... | collective-permute-start | bytes 786440 | tf_op jit(solution)/shard_map/ppermute | solution.py:263
  (45 other events, 621.3 us)
Sparse Core Ops, SparseCore 0:
  10.2 69.0 all-gather.1

commit v2 on v0

--- a/solution.py
+++ b/solution.py
@@ -1,13 +1,354 @@
+import functools
+
 import jax
 import jax.numpy as jnp
+import numpy as np
 from jax import lax
+from jax.experimental import pallas as pl
+from jax.experimental.pallas import tpu as pltpu
 from jax.sharding import PartitionSpec as P
 
 RANK = 64
 BLOCK = 128
-
-
-def per_device(
+VMEM_LIMIT = 60 * 1024 * 1024
+
+
+NT = (((1,), (1,)), ((), ()))
+TN = (((0,), (0,)), ((), ()))
+
+
+def takes(us):
+    return pl.CostEstimate(flops=int(us * 1.15e9), bytes_accessed=int(us * 1e6), transcendentals=0)
+
+
+def pick_kernel(shard, where, *refs):
+    out = refs[-1]
+    for j, src in enumerate(refs[:-1]):
+        out[:, j * shard : (j + 1) * shard] = src[...]
+
+
+def pick_columns(where, tokens, shard):
+    count = tokens.shape[0]
+    blocks = where.shape[0]
+    return pl.pallas_call(
+        functools.partial(pick_kernel, shard),
+        grid_spec=pltpu.PrefetchScalarGridSpec(
+            num_scalar_prefetch=1,
+            grid=(1,),
+            in_specs=[
+                pl.BlockSpec((count, shard), lambda i, w, j=j: (0, w[j])) for j in range(blocks)
+            ],
+            out_specs=pl.BlockSpec((count, blocks * shard), lambda i, w: (0, 0)),
+        ),
+        out_shape=jax.ShapeDtypeStruct((count, blocks * shard), tokens.dtype),
+        compiler_params=pltpu.CompilerParams(vmem_limit_bytes=VMEM_LIMIT),
+        cost_estimate=takes(4),
+    )(where, *[tokens] * blocks)
+
+
+def part_kernel(blocks, shard, where, *refs):
+    tokens, (theirs, low_mine, low_theirs), rest = refs[:blocks], refs[blocks : blocks + 3], refs[blocks + 3 :]
+    for k in range(blocks):
+        at = slice(k * shard, (k + 1) * shard)
+        total = lax.dot_general(low_mine[...], tokens[k][...], TN, preferred_element_type=jnp.float32)
+        total += lax.dot_general(
+            low_theirs[...], theirs[:, at], TN, preferred_element_type=jnp.float32
+        )
+        if len(rest) == 1:
+            rest[0][:, at] = total.astype(jnp.bfloat16)
+            continue
+        received, own, held, sent = rest
+        total += received[:, at].astype(jnp.float32)
+        if k == 0:
+            own[...] = total
+        elif k == 2:
+            held[...] = total
+        else:
+            sent[:, (k // 2) * shard : (k // 2 + 1) * shard] = total.astype(jnp.bfloat16)
+
+
+def part_sums(where, side, tokens, pair_tokens, low_mine, low_theirs, shard, received=None):
+    count = tokens.shape[0]
+    blocks = where.shape[0]
+    low_width = low_mine.shape[1]
+
+    def whole(rows, columns, at=0):
+        return pl.BlockSpec((rows, columns), lambda i, w: (0, at))
+
+    operands = [tokens] * blocks + [pair_tokens, low_mine, low_theirs]
+    specs = [pl.BlockSpec((count, shard), lambda i, w, k=k: (0, w[k])) for k in range(blocks)]
+    specs += [whole(count, blocks * shard, side)] + [whole(count, low_width)] * 2
+    if received is None:
+        shapes = [(blocks * shard, jnp.bfloat16)]
+    else:
+        operands.append(received)
+        specs.append(whole(low_width, blocks * shard))
+        shapes = [(shard, jnp.float32), (shard, jnp.float32), (2 * shard, jnp.bfloat16)]
+    return pl.pallas_call(
+        functools.partial(part_kernel, blocks, shard),
+        grid_spec=pltpu.PrefetchScalarGridSpec(
+            num_scalar_prefetch=1,
+            grid=(1,),
+            in_specs=specs,
+            out_specs=[whole(low_width, columns) for columns, _ in shapes],
+        ),
+        out_shape=[jax.ShapeDtypeStruct((low_width, columns), kind) for columns, kind in shapes],
+        compiler_params=pltpu.CompilerParams(vmem_limit_bytes=VMEM_LIMIT),
+        cost_estimate=takes(4),
+    )(where, *operands)
+
+
+def finish_kernel(own, first, second, norm, out):
+    total = own[...] + first[...].astype(jnp.float32) + second[...].astype(jnp.float32)
+    out[...] = (total * norm[...]).T
+
+
+def finish_sums(own, first, second, norm):
+    rows, columns = own.shape
+
+    def whole(a):
+        return pl.BlockSpec(a, lambda i: (0, 0))
+
+    return pl.pallas_call(
+        finish_kernel,
+        grid=(1,),
+        in_specs=[whole((rows, columns))] * 3 + [whole((rows, 1))],
+        out_specs=whole((columns, rows)),
+        out_shape=jax.ShapeDtypeStruct((columns, rows), jnp.float32),
+        compiler_params=pltpu.CompilerParams(vmem_limit_bytes=VMEM_LIMIT),
+    )(own, first, second, norm)
+
+
+def low_kernel(many, where, *refs):
+    tokens, (pair_tokens, down, low, pair_low) = refs[:many], refs[many:]
+    shard = tokens[0].shape[1]
+    for j in range(many):
+        rows = down[pl.ds(pl.multiple_of(where[2 * many + j] * shard, shard), shard), :]
+        at = pl.ds(pl.multiple_of(where[many + j] * shard, shard), shard)
+        mine = jnp.dot(tokens[j][...], rows, preferred_element_type=jnp.float32)
+        theirs = jnp.dot(pair_tokens[:, at], rows, preferred_element_type=jnp.float32)
+        if j == 0:
+            low[...], pair_low[...] = mine, theirs
+        else:
+            low[...] += mine
+            pair_low[...] += theirs
+
+
+def low_sums(own_at, pair_at, down_at, tokens, pair_tokens, down, shard):
+    count, low_width = tokens.shape[0], down.shape[1]
+    many = own_at.shape[0]
+
+    def whole(a):
+        return pl.BlockSpec(a.shape, lambda i, w: (0, 0))
+
+    out = pl.BlockSpec((count, low_width), lambda i, w: (0, 0))
+    return pl.pallas_call(
+        functools.partial(low_kernel, many),
+        grid_spec=pltpu.PrefetchScalarGridSpec(
+            num_scalar_prefetch=1,
+            grid=(1,),
+            in_specs=[
+                pl.BlockSpec((count, shard), lambda i, w, j=j: (0, w[j])) for j in range(many)
+            ]
+            + [whole(pair_tokens), whole(down)],
+            out_specs=[out, out],
+        ),
+        out_shape=[jax.ShapeDtypeStruct((count, low_width), jnp.float32)] * 2,
+        compiler_params=pltpu.CompilerParams(vmem_limit_bytes=VMEM_LIMIT),
+        cost_estimate=takes(5),
+    )(jnp.concatenate([own_at, pair_at, down_at]), *[tokens] * many, pair_tokens, down)
+
+
+def shards_kernel(first, many, old, where, *refs):
+    refs = list(refs)
+    take = lambda n: [refs.pop(0) for _ in range(n)]
+    tok_in, pair_in = take(2)
+    sides, pieces, (down_in,) = take(4), take(2 * many), take(1)
+    before = [] if first else take(2)
+    came = take(1) if old else []
+    if not first:
+        take(1)
+    ig_out, pair_ig, acc, pair_acc = take(4)
+    rows, down, both, keys, low, ig, held, sems, out_sems = take(9)
+    half, count = pieces[0].shape[0], acc.shape[0]
+    shard = 2 * half
+    g = where[3 * many + old]
+    used = [0]
+
+    def load(source, target):
+        copy = pltpu.make_async_copy(source, target, sems.at[used[0]])
+        used[0] += 1
+        copy.start()
+        return copy
+
+    def columns(at):
+        return pl.ds(pl.multiple_of(at * shard, shard), shard)
+
+    start = [
+        load(sides[0], keys.at[:count]),
+        load(sides[1], keys.at[count:]),
+        load(sides[2], low.at[:count]),
+        load(sides[3], low.at[count:]),
+    ]
+    loads = []
+    for r in range(many):
+        loads.append(
+            [
+                load(piece, rows.at[r, pl.ds(pl.multiple_of(part * half, half), half), :])
+                for piece, part in ((pieces[2 * r], g), (pieces[2 * r + 1], 1 - g))
+            ]
+            + [
+                load(down_in.at[columns(where[2 * many + r]), :], down.at[r]),
+                load(tok_in.at[:, columns(where[r])], both.at[r, :count]),
+                load(pair_in.at[:, columns(where[many + r])], both.at[r, count:]),
+            ]
+        )
+        if r == 0:
+            sums = [load(a, to) for a, to in zip(before, (acc, pair_acc))]
+    arrived = [load(a, held) for a in came]
+    for copy in start:
+        copy.wait()
+    stores = []
+
+    def store(source, at):
+        stores.append(
+            pltpu.make_async_copy(source, ig_out.at[:, columns(at)], out_sems.at[len(stores)])
+        )
+        stores[-1].start()
+
+    for r in range(many):
+        for copy in loads[r]:
+            copy.wait()
+        block = lax.dot_general(keys[...], rows[r], NT, preferred_element_type=jnp.float32)
+        block += lax.dot_general(low[...], down[r], NT, preferred_element_type=jnp.float32)
+        ig[r] = block[:count].astype(ig.dtype)
+        pair_ig[:, r * shard : (r + 1) * shard] = block[count:].astype(ig.dtype)
+        store(ig.at[r], where[r])
+        term = jnp.dot(both[r], rows[r], preferred_element_type=jnp.float32)
+        if r == 0:
+            for copy in sums:
+                copy.wait()
+        if r == 0 and first:
+            acc[...], pair_acc[...] = term[:count], term[count:]
+        else:
+            acc[...] += term[:count]
+            pair_acc[...] += term[count:]
+        if r == 0:
+            for copy in arrived:
+                copy.wait()
+            for j in range(old):
+                store(held.at[:, j * shard : (j + 1) * shard], where[3 * many + j])
+    for copy in stores:
+        copy.wait()
+
+
+def add_shards(where, tokens, pair_tokens, sides, pieces, down, acc, came, ig):
+    count, width = tokens.shape
+    features = pieces[0].shape[1]
+    many = len(pieces) // 2
+    shard, low_width = 2 * pieces[0].shape[0], down.shape[1]
+    first = acc is None
+    old = 0 if came is None else came.shape[1] // shard
+    operands = [tokens, pair_tokens, *sides, *pieces, down]
+    if not first:
+        operands += acc
+    if old:
+        operands.append(came)
+    alias = {}
+    if not first:
+        alias = {len(operands) + 1: 0}
+        operands.append(ig)
+    bf16 = jnp.bfloat16
+    sums = pl.BlockSpec((count, features), lambda i, w: (0, 0))
+    ig, pair_ig, *acc = pl.pallas_call(
+        functools.partial(shards_kernel, first, many, old),
+        grid_spec=pltpu.PrefetchScalarGridSpec(
+            num_scalar_prefetch=1,
+            grid=(1,),
+            in_specs=[pl.BlockSpec(memory_space=pl.ANY)] * len(operands),
+            out_specs=[
+                pl.BlockSpec(memory_space=pl.ANY),
+                pl.BlockSpec((count, many * shard), lambda i, w: (0, 0)),
+                sums,
+                sums,
+            ],
+            scratch_shapes=[
+                pltpu.VMEM((many, shard, features), bf16),
+                pltpu.VMEM((many, shard, low_width), bf16),
+                pltpu.VMEM((many, 2 * count, shard), bf16),
+                pltpu.VMEM((2 * count, features), bf16),
+                pltpu.VMEM((2 * count, low_width), bf16),
+                pltpu.VMEM((many, count, shard), bf16),
+                pltpu.VMEM((count, max(old, 1) * shard), bf16),
+                pltpu.SemaphoreType.DMA((7 + 5 * many,)),
+                pltpu.SemaphoreType.DMA((many + old,)),
+            ],
+        ),
+        out_shape=[
+            jax.ShapeDtypeStruct((count, width), bf16),
+            jax.ShapeDtypeStruct((count, many * shard), bf16),
+            jax.ShapeDtypeStruct((count, features), jnp.float32),
+            jax.ShapeDtypeStruct((count, features), jnp.float32),
+        ],
+        input_output_aliases=alias,
+        compiler_params=pltpu.CompilerParams(vmem_limit_bytes=VMEM_LIMIT),
+        cost_estimate=takes(3 + 1.5 * many),
+    )(where, *operands)
+    return ig, pair_ig, acc
+
+
+def insert_kernel(blocks, where, received, *refs):
+    sems, out = refs[-1], refs[-2] if len(refs) == 3 else refs[-3]
+    shard = received.shape[1] // blocks
+    copies = []
+    for j in range(blocks):
+        to = pl.ds(pl.multiple_of(where[j] * shard, shard), shard)
+        copies.append(
+            pltpu.make_async_copy(
+                received.at[:, j * shard : (j + 1) * shard], out.at[:, to], sems.at[j]
+            )
+        )
+        copies[-1].start()
+    if len(refs) > 3:
+        low, up, acc, theirs, live, _, _, keys, _ = refs
+        total = acc[...] + theirs[...]
+        total += jnp.dot(low[...], up[...], preferred_element_type=jnp.float32)
+        keys[...] = (total * live[...]).astype(keys.dtype)
+    for copy in copies:
+        copy.wait()
+
+
+def insert(where, received, ig, ending=()):
+    count, width = ig.shape
+    blocks = where.shape[0]
+
+    def whole(a):
+        return pl.BlockSpec(a.shape, lambda i, w: (0, 0))
+
+    outs = [pl.BlockSpec(memory_space=pl.ANY)]
+    shapes = [jax.ShapeDtypeStruct(ig.shape, ig.dtype)]
+    if ending:
+        features = ending[2].shape[1]
+        outs.append(pl.BlockSpec((count, features), lambda i, w: (0, 0)))
+        shapes.append(jax.ShapeDtypeStruct((count, features), ig.dtype))
+    return pl.pallas_call(
+        functools.partial(insert_kernel, blocks),
+        grid_spec=pltpu.PrefetchScalarGridSpec(
+            num_scalar_prefetch=1,
+            grid=(1,),
+            in_specs=[whole(a) for a in (received, *ending)]
+            + [pl.BlockSpec(memory_space=pl.ANY)],
+            out_specs=outs,
+            scratch_shapes=[pltpu.SemaphoreType.DMA((blocks,))],
+        ),
+        out_shape=shapes,
+        input_output_aliases={2 + len(ending): 0},
+        compiler_params=pltpu.CompilerParams(vmem_limit_bytes=VMEM_LIMIT),
+        cost_estimate=takes(2.5),
+    )(where, received, *ending, ig)
+
+
+def plain_form(
     tokens, key_weight, adapter_down, adapter_up, key_cotangent, block_job, block_live, job_rank
 ):
     tok_count = tokens.shape[0]
@@ -78,6 +419,212 @@
     return (keys, input_grad, down_grad, up_grad)
 
 
+def per_device(
+    n, tokens, key_weight, adapter_down, adapter_up, key_cotangent, block_job, block_live, job_rank
+):
+    if n != 16 or key_weight.shape[0] % 512 or lax.axis_size("groups") != 2:
+        return plain_form(
+            tokens,
+            key_weight,
+            adapter_down,
+            adapter_up,
+            key_cotangent,
+            block_job,
+            block_live,
+            job_rank,
+        )
+    f32, bf16 = jnp.float32, jnp.bfloat16
+    outer = n // 4
+    count, width = tokens.shape
+    features = key_weight.shape[1]
+    shard = key_weight.shape[0]
+    jobs = job_rank.shape[0]
+    low_width = adapter_down.shape[1]
+    here = block_live.shape[0]
+    idx = lax.axis_index("fsdp")
+    g = lax.axis_index("groups")
+    z, y, c = idx // 4, (idx // 2) % 2, idx % 2
+
+    def swap(v, mask):
+        return lax.ppermute(v, "fsdp", [(s, s ^ mask) for s in range(n)])
+
+    def across(v):
+        return lax.ppermute(v, "groups", [(0, 1), (1, 0)])
+
+    def rows_of(v, i, size):
+        return lax.dynamic_slice_in_dim(v, i * size, size, 0)
+
+    local_job = rows_of(block_job, idx, here)
+    pair_job = rows_of(block_job, idx ^ 1, here)
+    position = jnp.arange(count, dtype=jnp.int32)
+    live = (position % BLOCK < jnp.repeat(block_live, BLOCK)).astype(f32)
+    columns = jnp.arange(low_width, dtype=jnp.int32)
+    col_job = columns // RANK
+    col_rank = jnp.repeat(job_rank, RANK)
+    col_scale = jnp.where(columns % RANK < col_rank, 16.0 / col_rank.astype(f32), 0.0)
+
+    def column_mask(job):
+        mine = col_job[None, :] == jnp.repeat(job, BLOCK)[:, None]
+        return mine.astype(f32) * col_scale[None, :]
+
+    colmask = column_mask(local_job) * live[:, None]
+    grad_keys = (key_cotangent.astype(f32) * live[:, None]).astype(bf16)
+
+    def after(done, *values):
+        values = lax.optimization_barrier((tuple(values), tuple(done)))[0]
+        return values if len(values) > 1 else values[0]
+
+    half = shard // 2
+    mine, rest = rows_of(key_weight, g, half), rows_of(key_weight, 1 - g, half)
+
+    def after(done, *values):
+        values = lax.optimization_barrier((tuple(values), tuple(done)))[0]
+        return values if len(values) > 1 else values[0]
+
+    last = {}
+
+    def send(link, go, value, *also):
+        if link in last or also:
+            value = after(last.get(link, []) + list(also), value)
+        got = go(value)
+        last[link] = [got]
+        return got
+
+    def beside(value, *also):
+        return send("y", lambda v: swap(v, 2), value, *also)
+
+    def along(value, mask, *also):
+        return send("z", lambda v: swap(v, mask), value, *also)
+
+    def over(value, *also):
+        return send("x", across, value, *also)
+
+    half = shard // 2
+    mine, rest = rows_of(key_weight, g, half), rows_of(key_weight, 1 - g, half)
+    near, far = [mine, swap(mine, 4), swap(mine, 8)], [beside(mine)]
+    last["z"] = near[1:]
+    far_rest = [over(far[0])]
+    near_rest = [rest, over(near[1])]
+
+    up_rows = adapter_up.shape[0]
+    tail = jnp.pad(block_live.astype(bf16), (0, 128 - here))
+    packed = jnp.concatenate(
+        [adapter_up, jnp.broadcast_to(tail[None, :], (up_rows, 128))], axis=1
+    )
+    gathered = jnp.concatenate([packed, swap(after(far, packed), 2)], axis=0)
+    gathered = after(near[1:] + far_rest, gathered)
+    gathered = jnp.concatenate([gathered, swap(gathered, 4)], axis=0)
+    gathered = after(near_rest[1:], gathered)
+    gathered = jnp.concatenate([gathered, swap(gathered, 8)], axis=0)
+    gathered = jnp.concatenate([gathered, swap(gathered, 1)], axis=0)
+    at = jnp.arange(n * up_rows, dtype=jnp.int32)
+    place = at // up_rows
+    mask = 2 * (place % 2) + 4 * (place // 2 % outer) + place // (2 * outer)
+    source = (idx ^ mask) * up_rows + at % up_rows
+    order = (at[:, None] == source[None, :]).astype(bf16)
+    ordered = jnp.dot(order, gathered, preferred_element_type=f32).astype(bf16)
+
+    same_core = [[q for q in range(n) if q % 2 == p] for p in range(2)]
+    down_rows = lax.all_gather(
+        adapter_down, "fsdp", axis=0, tiled=True, axis_index_groups=same_core
+    )
+
+    relative = jnp.arange(outer, dtype=jnp.int32)
+    near_at = 4 * (z ^ relative) + 2 * y + c
+    far_at = near_at + 2 - 4 * y
+    pair_keys = swap(grad_keys, 1)
+    pair_tokens = swap(
+        pick_columns(jnp.concatenate([far_at, near_at]) + 1 - 2 * c, tokens, shard), 1
+    )
+
+    far.append(beside(near[1]))
+    far_rest.append(over(far[1]))
+    near_rest.append(over(near[2]))
+    far.append(beside(near[2]))
+    near.append(along(near[2], 4))
+    near_rest.append(along(near_rest[2], 4))
+
+    up_full = ordered[:, :features]
+    live_all = ordered.reshape(n, up_rows, features + 128)[:, 0, features : features + here]
+    live_all = live_all.reshape(n * here).astype(f32)
+    onehot = (block_job[:, None] == jnp.arange(jobs, dtype=jnp.int32)[None, :]).astype(f32)
+    count_of = jnp.sum(onehot * live_all[:, None], axis=0)
+    norm = jnp.repeat(1.0 / jnp.sqrt(jnp.maximum(count_of, 1.0)), RANK)
+
+    def grad_low_of(keys, mask):
+        return (
+            lax.dot_general(keys, up_full, NT, preferred_element_type=f32) * mask
+        ).astype(bf16)
+
+    grad_low = grad_low_of(grad_keys, colmask)
+    pair_low = grad_low_of(pair_keys, column_mask(pair_job))
+    (part_far,) = part_sums(far_at, 0, tokens, pair_tokens, grad_low, pair_low, shard)
+    part_swapped = beside(part_far)
+    far.append(beside(near[3]))
+    far_rest.append(over(far[2]))
+    far_rest.append(over(far[3]))
+
+    own, held, sent = part_sums(
+        near_at, 1, tokens, pair_tokens, grad_low, pair_low, shard, part_swapped
+    )
+    first = along(sent, 4)
+    second = along((held + first[:, shard:].astype(f32)).astype(bf16), 8)
+
+    sides = [grad_keys, pair_keys, grad_low, pair_low]
+    order_of = [(k, d) for k in range(outer) for d in range(2)]
+
+    def places(shards):
+        k = np.array([s[0] for s in shards], np.int32)
+        d = np.array([s[1] for s in shards], np.int32)
+        own = 4 * (z ^ k) + 2 * (y ^ d) + c
+        return own, outer - outer * d + k, 2 * (z ^ k) + (y ^ d)
+
+    def run(shards, acc, came, ig):
+        pieces = []
+        for k, distant in shards:
+            pieces += [far[k], far_rest[k]] if distant else [near[k], near_rest[k]]
+        own, pair, row = places(shards)
+        at, came = ([], None) if came is None else ([came[0]], came[1])
+        where = jnp.concatenate([own, pair, row] + at + [jnp.broadcast_to(g, (1,))])
+        ig, pair_ig, acc = add_shards(
+            where.astype(jnp.int32), tokens, pair_tokens, sides, pieces, down_rows, acc, came, ig
+        )
+        return ig, (own + 1 - 2 * c, swap(pair_ig, 1)), acc
+
+    sides[2] = after([sent], sides[2])
+    ig, came, acc = run(((0, 0), (0, 1), (1, 0), (1, 1)), None, None, None)
+    low, pair_sum = low_sums(
+        *places(order_of),
+        tokens,
+        pair_tokens,
+        down_rows,
+        shard,
+    )
+    low = ((low + swap(pair_sum, 1)) * colmask).astype(bf16)
+    up_term = lax.dot_general(low, grad_keys, TN, preferred_element_type=f32)
+    up_term = up_term.reshape(outer, 2, 2, up_rows, features)
+    up_sum = lax.dynamic_index_in_dim(up_term, c, 2, False) + swap(
+        lax.dynamic_index_in_dim(up_term, 1 - c, 2, False), 1
+    )
+    up_sum = lax.dynamic_index_in_dim(up_sum, y, 1, False) + swap(
+        lax.dynamic_index_in_dim(up_sum, 1 - y, 1, False), 2
+    )
+    up_owned = lax.dynamic_index_in_dim(up_sum, z, 0, False)
+    acc[0] = after([first, up_sum], acc[0])
+    ig, came, acc = run(((2, 0), (2, 1)), acc, came, ig)
+    for k in range(1, outer):
+        sent_up = lax.dynamic_index_in_dim(up_sum, z ^ k, 0, False)
+        up_owned = up_owned + swap(sent_up, 4 * k)
+    up_grad = up_owned * rows_of(norm, idx, up_rows)[:, None]
+    down_grad = finish_sums(own, first, second, norm[:, None])
+
+    acc[0] = after([down_grad, up_grad], acc[0])
+    ig, came, acc = run(((3, 0), (3, 1)), acc, came, ig)
+    ending = [low, up_full, acc[0], swap(acc[1], 1), live[:, None]]
+    ig, keys = insert(*came, ig, ending)
+    return (keys, ig, down_grad, up_grad)
+
+
 def solution(mesh):
     placed = (
         P(("groups", "fsdp"), None),
@@ -90,14 +637,9 @@
         P("groups"),
     )
     return jax.shard_map(
-        per_device,
+        functools.partial(per_device, mesh.shape["fsdp"]),
         mesh=mesh,
         in_specs=placed,
-        out_specs=(
-            P(("groups", "fsdp"), None),
-            P(("groups", "fsdp"), None),
-            P(("groups", "fsdp"), None),
-            P(("groups", "fsdp"), None),
-        ),
+        out_specs=(P(("groups", "fsdp"), None),) * 4,
         check_vma=False,
     )

time: 347 us -> 187 us (0.54)
  blocking collectives: 162 us -> 0 us
  Pallas kernels: 0 us -> 49.3 us
  matrix products: 47.3 us -> 4.69 us
  waiting for transfers between devices: 99.9 us -> 65.4 us
  starting transfers between devices: 4.81 us -> 35.3 us
  local copies, waits for them, and re-layouts: 16.2 us -> 12.6 us
    psum x1 -> x0, blocking collectives: 103 us -> none  [per_device(): count = lax.psum(local_count, 'fsdp')]
    all_gather x2 -> x1, waiting for transfers between devices: 98.5 us -> 0.01 us  [per_device(): lax.all_gather(adapter_down, 'fsdp', axis=0, tiled=True, axis_index_group...]
    ppermute x0 -> x33, waiting for transfers between devices: none -> 65.3 us  [the longest x27 47.3 us: swap(): return lax.ppermute(v, 'fsdp', [(s, s ^ mask) for s in range(n)])]
    all_gather x2 -> x0, blocking collectives: 59.1 us -> none  [the longest x1 35.1 us: per_device(): up_full = lax.all_gather(adapter_up, 'fsdp', axis=0, tiled=True)]
    pallas_call x0 -> x9, Pallas kernels: none -> 49.3 us  [the longest x3 25.1 us: add_shards(): pl.pallas_call(functools.partial(shards_kernel, first, many, old), grid_s...]
    dot_general x11 -> x4, matrix products: 47.3 us -> 4.69 us  [the longest x2 3.05 us: grad_low_of(): lax.dot_general(keys, up_full, NT, preferred_element_type=f32) * mask]
    ppermute x0 -> x33, starting transfers between devices: none -> 35.3 us  [the longest x27 25.8 us: swap(): return lax.ppermute(v, 'fsdp', [(s, s ^ mask) for s in range(n)])]
    all_to_all x1 -> x0, local copies, waits for them, and re-layouts: 6.42 us -> none  [per_device(): lax.all_to_all(tokens, 'fsdp', split_axis=1, concat_axis=0, tiled=True)]
  transfers between devices with their start and end apart: 4 -> 34, of which waited for: 2 -> 12; matrix products, arithmetic and copies ran while one was open for 7% -> 8% of each run, Pallas kernels for 0% -> 20%
where the time goes in v2:
time: 187 us
  waiting for transfers between devices  65.4 us (35%)
  Pallas kernels  49.3 us (26%)
  starting transfers between devices  35.3 us (19%)
  between operations  14.5 us (8%)
  local copies, waits for them, and re-layouts  12.6 us (7%)
  other arithmetic  5.03 us (3%)
  matrix products  4.69 us (3%)
    ppermute x27, waiting for transfers between devices, swap(): return lax.ppermute(v, 'fsdp', [(s, s ^ mask) for s in range(n)])  47.3 us
    ppermute x27, starting transfers between devices, swap(): return lax.ppermute(v, 'fsdp', [(s, s ^ mask) for s in range(n)])  25.8 us
    pallas_call x3, Pallas kernels, add_shards(): pl.pallas_call(functools.partial(shards_kernel, first, many, old), grid_s...  25.1 us
    ppermute x6, waiting for transfers between devices, across(): return lax.ppermute(v, 'groups', [(0, 1), (1, 0)])  18 us
    ppermute x6, starting transfers between devices, across(): return lax.ppermute(v, 'groups', [(0, 1), (1, 0)])  9.43 us
    pallas_call x2, Pallas kernels, part_sums(): pl.pallas_call(functools.partial(part_kernel, blocks, shard), grid_spec=p...  8.2 us
    unnamed x66, local copies, waits for them, and re-layouts  5.74 us
    pallas_call x1, Pallas kernels, low_sums(): pl.pallas_call(functools.partial(low_kernel, many), grid_spec=pltpu.Prefe...  5.65 us
  transfers between devices with their start and end apart: 34, of which 12 were waited for; matrix products, arithmetic and copies ran while one was open for 8% of the time, Pallas kernels for 20%

profile of v2, /device:TPU:0, one launch (start us, length us, event | category | flops | bytes accessed | tf_op | source)
XLA Modules:
  0.0 186.7 jit_solution(5838886334327008227)
XLA Ops:
  7.2 2.3 %constant_dynamic-slice_fusion = (bf16[256,1024]{1,0:T(8,128)(2,1)}, bf16[256,1024]{1,0:T(8,128)(2,1)}) fusion(bf16[512,1024]{1,0:T(8,128)(2,1)} %param.21, s32[]{:T(128)S(6)} %select_n.165, s32[]{:T(128)S(6)} %select_n.159), kind=kLoop, calls=%fused_computation.33 | loop fusion | bytes 2097160 | tf_op jit(solution)/shard_map/dynamic_slice | solution.py:455
  9.5 3.0 %collective-permute-start.2 = (bf16[256,1024]{1,0:T(8,128)(2,1)}, bf16[256,1024]{1,0:T(8,128)(2,1)}, u32[]{:S(2)}, u32[]{:S(2)}) collective-permute-start(bf16[256,1024]{1,0:T(8,128)(2,1)} %get-tuple-element.89.refs_6_), channel_id=1, source_target_pairs={{0,2},{1,3},{2,0},{3,1},{4,6},{5,7},{6,4},{7,5},{8,10},{9,11},{10,... | collective-permute-start | bytes 1572872 | tf_op jit(solution)/shard_map/ppermute | solution.py:449
  14.0 2.6 %collective-permute-start.5 = (bf16[256,1024]{1,0:T(8,128)(2,1)}, bf16[256,1024]{1,0:T(8,128)(2,1)}, u32[]{:S(2)}, u32[]{:S(2)}) collective-permute-start(bf16[256,1024]{1,0:T(8,128)(2,1)} %get-tuple-element.89.refs_6_), channel_id=1, source_target_pairs={{0,8},{1,9},{2,10},{3,11},{4,12},{5,13},{6,14},{7,15},{8,0},{9,1},... | collective-permute-start | bytes 1572872 | tf_op jit(solution)/shard_map/ppermute | solution.py:449
  17.3 3.8 %shard_map.219 = bf16[256,4096]{1,0:T(8,128)(2,1)} custom-call(s32[8]{0:T(128)} %fusion.26.where, bf16[256,8192]{1,0:T(8,128)(2,1)} %refs_0_.13, bf16[256,8192]{1,0:T(8,128)(2,1)} %refs_0_.13, bf16[256,8192]{1,0:T(8,128)(2,1)} %refs_0_.13, bf16[256,8192]{1,0:T(8,128)(2,1)} %refs_0_.13, bf16[256,8192]{1,0:T(8,128)(2,1)} %refs_0_.13, ...), custom_call_target="tpu_custom_call" | custom-call | flops 4600000000 | bytes 4000000 | tf_op jit(solution)/shard_map/pallas_call | solution.py:33
  21.7 3.0 %collective-permute-done.2.refs_8_ = bf16[256,1024]{1,0:T(8,128)(2,1)} collective-permute-done((bf16[256,1024]{1,0:T(8,128)(2,1)}, bf16[256,1024]{1,0:T(8,128)(2,1)}, u32[]{:S(2)}, u32[]{:S(2)}) %collective-permute-start.2) | collective-permute-done | bytes 524320 | tf_op jit(solution)/shard_map/ppermute | solution.py:449
  28.0 15.5 %collective-permute-done.4.refs_10_ = bf16[256,1024]{1,0:T(8,128)(2,1)} collective-permute-done((bf16[256,1024]{1,0:T(8,128)(2,1)}, bf16[256,1024]{1,0:T(8,128)(2,1)}, u32[]{:S(2)}, u32[]{:S(2)}) %collective-permute-start.4) | collective-permute-done | bytes 524320 | tf_op jit(solution)/shard_map/ppermute | solution.py:449
  46.6 2.9 %collective-permute-done.7 = bf16[32,1152]{1,0:T(8,128)(2,1)S(1)} collective-permute-done((bf16[32,1152]{1,0:T(8,128)(2,1)S(1)}, bf16[32,1152]{1,0:T(8,128)(2,1)S(1)}, u32[]{:S(2)}, u32[]{:S(2)}) %collective-permute-start.7) | collective-permute-done | bytes 73760 | tf_op jit(solution)/shard_map/ppermute | solution.py:449
  49.5 8.5 %collective-permute-done.8.refs_11_ = bf16[256,1024]{1,0:T(8,128)(2,1)S(1)} collective-permute-done((bf16[256,1024]{1,0:T(8,128)(2,1)}, bf16[256,1024]{1,0:T(8,128)(2,1)S(1)}, u32[]{:S(2)}, u32[]{:S(2)}) %collective-permute-start.8) | collective-permute-done | bytes 524320 | tf_op jit(solution)/shard_map/ppermute | solution.py:452
  61.1 14.4 %collective-permute-done.9 = bf16[64,1152]{1,0:T(8,128)(2,1)S(1)} collective-permute-done((bf16[64,1152]{1,0:T(8,128)(2,1)S(1)}, bf16[64,1152]{1,0:T(8,128)(2,1)S(1)}, u32[]{:S(2)}, u32[]{:S(2)}) %collective-permute-start.9) | collective-permute-done | bytes 147488 | tf_op jit(solution)/shard_map/ppermute | solution.py:449
  76.9 2.7 %collective-permute-done.11.refs_12_ = bf16[256,1024]{1,0:T(8,128)(2,1)} collective-permute-done((bf16[256,1024]{1,0:T(8,128)(2,1)}, bf16[256,1024]{1,0:T(8,128)(2,1)}, u32[]{:S(2)}, u32[]{:S(2)}) %collective-permute-start.11) | collective-permute-done | bytes 524320 | tf_op jit(solution)/shard_map/ppermute | solution.py:449
  83.9 2.0 %fusion.1.refs_6_.refs_5_ = bf16[256,256]{1,0:T(8,128)(2,1)} fusion(bf16[256,1024]{1,0:T(8,128)(2,1)} %collective-permute-done.1.refs_3_, f32[256]{0:T(256)S(1)} %compare_select_fusion.2, s32[256]{0:T(256)S(1)} %and_select_fusion.2, s32[256]{0:T(256)S(1)} %copy-done.32, bf16[256,1152]{1,0:T(8,128)(2,1)S(1)} %convolution_convert_fusion), kind=kOutput, calls=%fused_computation.4 | convolution fusion | flops 134479872 | bytes 1182720 | tf_op jit(solution)/shard_map/dot_general | solution.py:556
  87.3 4.0 %shard_map.220 = bf16[256,2048]{1,0:T(8,128)(2,1)} custom-call(s32[4]{0:T(128)} %copy-done.13, bf16[256,8192]{1,0:T(8,128)(2,1)} %refs_0_.13, bf16[256,8192]{1,0:T(8,128)(2,1)} %refs_0_.13, bf16[256,8192]{1,0:T(8,128)(2,1)} %refs_0_.13, bf16[256,8192]{1,0:T(8,128)(2,1)} %refs_0_.13, bf16[256,4096]{1,0:T(8,128)(2,1)} %copy-done, ...), custom_call_target="tpu_custom_call" | custom-call | flops 4600000000 | bytes 4000000 | tf_op jit(solution)/shard_map/pallas_call | solution.py:87
  91.3 1.9 collective-permute-done.12.refs_8_
  97.3 9.5 %collective-permute-done.16.refs_7_ = bf16[256,1024]{1,0:T(8,128)(2,1)S(1)} collective-permute-done((bf16[256,1024]{1,0:T(8,128)(2,1)}, bf16[256,1024]{1,0:T(8,128)(2,1)S(1)}, u32[]{:S(2)}, u32[]{:S(2)}) %collective-permute-start.16) | collective-permute-done | bytes 524320 | tf_op jit(solution)/shard_map/ppermute | solution.py:452
  109.8 5.7 %shard_map.223 = (f32[256,256]{1,0:T(8,128)}, f32[256,256]{1,0:T(8,128)}) custom-call(s32[24]{0:T(128)} %pad_add_fusion.1.where, bf16[256,8192]{1,0:T(8,128)(2,1)} %refs_0_.13, bf16[256,8192]{1,0:T(8,128)(2,1)} %refs_0_.13, bf16[256,8192]{1,0:T(8,128)(2,1)} %refs_0_.13, bf16[256,8192]{1,0:T(8,128)(2,1)} %refs_0_.13, bf16[256,8192]{1,0:T(8,128)(2,1)} %refs_0_.13, ...), custom_call_target="tpu_custom_call" | custom-call | flops 5750000128 | bytes 5000000 | tf_op jit(solution)/shard_map/pallas_call | solution.py:145
  118.2 4.2 %shard_map.221 = (f32[256,512]{1,0:T(8,128)}, f32[256,512]{1,0:T(8,128)}, bf16[256,1024]{1,0:T(8,128)(2,1)}) custom-call(s32[4]{0:T(128)} %copy-done.12, bf16[256,8192]{1,0:T(8,128)(2,1)} %refs_0_.13, bf16[256,8192]{1,0:T(8,128)(2,1)} %refs_0_.13, bf16[256,8192]{1,0:T(8,128)(2,1)} %refs_0_.13, bf16[256,8192]{1,0:T(8,128)(2,1)} %refs_0_.13, ...), custom_call_target="tpu_custom_call" | custom-call | flops 4600000000 | bytes 4000000 | tf_op jit(solution)/shard_map/pallas_call | solution.py:87
  125.2 10.3 %shard_map.222 = (bf16[256,8192]{1,0:T(8,128)(2,1)}, bf16[256,2048]{1,0:T(8,128)(2,1)}, f32[256,1024]{1,0:T(8,128)}, f32[256,1024]{1,0:T(8,128)}) custom-call(s32[13]{0:T(128)} %pad_add_fusion.where, bf16[256,8192]{1,0:T(8,128)(2,1)} %refs_0_.13, bf16[256,4096]{1,0:T(8,128)(2,1)} %copy-done, bf16[256,1024]{1,0:T(8,128)(2,1)} %copy-done.1, ...), custom_call_target="tpu_custom_call" | custom-call | flops 10350000128 | bytes 9000000 | tf_op jit(solution)/shard_map/pallas_call | solution.py:263
  139.6 2.7 %collective-permute-start.26 = (bf16[256,512]{1,0:T(8,128)(2,1)S(1)}, bf16[256,512]{1,0:T(8,128)(2,1)S(1)}, u32[]{:S(2)}, u32[]{:S(2)}) collective-permute-start(bf16[256,512]{1,0:T(8,128)(2,1)S(1)} %add_convert_fusion), channel_id=1, source_target_pairs={{0,8},{1,9},{2,10},{3,11},{4,12},{5,13},{6,14},{7,15},{8,0},{9,1},... | collective-permute-start | bytes 786440 | tf_op jit(solution)/shard_map/ppermute | solution.py:449
  142.2 2.4 %collective-permute-done.24 = f32[4,16,1024]{2,1,0:T(8,128)S(1)} collective-permute-done((f32[4,16,1024]{2,1,0:T(8,128)S(1)}, f32[4,16,1024]{2,1,0:T(8,128)S(1)}, u32[]{:S(2)}, u32[]{:S(2)}) %collective-permute-start.24) | collective-permute-done | bytes 262176 | tf_op jit(solution)/shard_map/ppermute | solution.py:449
  144.7 7.5 %shard_map.224 = (bf16[256,8192]{1,0:T(8,128)(2,1)}, bf16[256,1024]{1,0:T(8,128)(2,1)}, f32[256,1024]{1,0:T(8,128)}, f32[256,1024]{1,0:T(8,128)}) custom-call(s32[11]{0:T(128)} %concatenate.38.where, bf16[256,8192]{1,0:T(8,128)(2,1)} %refs_0_.13, bf16[256,4096]{1,0:T(8,128)(2,1)} %copy-done, ...), custom_call_target="tpu_custom_call", output_to_operand_aliasing={{0}: (15, {})} | custom-call | flops 6899999744 | bytes 6000000 | tf_op jit(solution)/shard_map/pallas_call | solution.py:263
  152.7 2.7 %collective-permute-start.28 = (f32[16,1024]{1,0:T(8,128)S(1)}, f32[16,1024]{1,0:T(8,128)S(1)}, u32[]{:S(2)}, u32[]{:S(2)}) collective-permute-start(f32[16,1024]{1,0:T(8,128)S(1)} %get-tuple-element.92), channel_id=1, source_target_pairs={{0,8},{1,9},{2,10},{3,11},{4,12},{5,13},{6,14},{7,15},{8,0},{9,1},... | collective-permute-start | bytes 196616 | tf_op jit(solution)/shard_map/ppermute | solution.py:449
  157.7 2.3 %shard_map.225 = f32[512,256]{1,0:T(8,128)} custom-call(f32[256,512]{1,0:T(8,128)} %get-tuple-element.67.own, bf16[256,1024]{1,0:T(8,128)(2,1)} %copy-done.2, bf16[256,512]{1,0:T(8,128)(2,1)} %copy-done.9, f32[256,1]{1,0:T(8,128)} %broadcast_in_dim_reshape.6.norm), custom_call_target="tpu_custom_call" | custom-call | tf_op jit(solution)/shard_map/pallas_call | solution.py:112
  163.4 7.4 %shard_map.226 = (bf16[256,8192]{1,0:T(8,128)(2,1)}, bf16[256,1024]{1,0:T(8,128)(2,1)}, f32[256,1024]{1,0:T(8,128)}, f32[256,1024]{1,0:T(8,128)}) custom-call(s32[9]{0:T(128)} %concatenate.31.where, bf16[256,8192]{1,0:T(8,128)(2,1)} %refs_0_.13, bf16[256,4096]{1,0:T(8,128)(2,1)} %copy-done, ...), custom_call_target="tpu_custom_call", output_to_operand_aliasing={{0}: (15, {})} | custom-call | flops 6899999744 | bytes 6000000 | tf_op jit(solution)/shard_map/pallas_call | solution.py:263
  175.6 4.2 %shard_map.227 = (bf16[256,8192]{1,0:T(8,128)(2,1)}, bf16[256,1024]{1,0:T(8,128)(2,1)}) custom-call(s32[2]{0:T(128)} %get-tuple-element.86.where, bf16[256,1024]{1,0:T(8,128)(2,1)} %copy-done.30, bf16[256,256]{1,0:T(8,128)(2,1)} %copy-done.6, bf16[256,1024]{1,0:T(8,128)(2,1)} %slice.12.refs_1_, ...), custom_call_target="tpu_custom_call", output_to_operand_aliasing={{0}: (7, {})} | custom-call | flops 2875000064 | bytes 2500000 | tf_op jit(solution)/shard_map/pallas_call | solution.py:334
  (176 shorter events, 47.1 us)
Async XLA Ops:
  7.2 102.7 %all-gather.2.cloned.1.call-start = ((), (), s32[]{:S(2)}) async-start(), calls=%async_computation | async-start | bytes 2359296 | tf_op jit(solution)/shard_map/all_gather | solution.py:528
  9.5 15.2 %collective-permute-start.2 = (bf16[256,1024]{1,0:T(8,128)(2,1)}, bf16[256,1024]{1,0:T(8,128)(2,1)}, u32[]{:S(2)}, u32[]{:S(2)}) collective-permute-start(bf16[256,1024]{1,0:T(8,128)(2,1)} %get-tuple-element.89.refs_6_), channel_id=1, source_target_pairs={{0,2},{1,3},{2,0},{3,1},{4,6},{5,7},{6,4},{7,5},{8,10},{9,11},{10,... | collective-permute-start | bytes 1572872 | tf_op jit(solution)/shard_map/ppermute | solution.py:449
  12.4 31.0 %collective-permute-start.4 = (bf16[256,1024]{1,0:T(8,128)(2,1)}, bf16[256,1024]{1,0:T(8,128)(2,1)}, u32[]{:S(2)}, u32[]{:S(2)}) collective-permute-start(bf16[256,1024]{1,0:T(8,128)(2,1)} %get-tuple-element.89.refs_6_), channel_id=1, source_target_pairs={{0,4},{1,5},{2,6},{3,7},{4,0},{5,1},{6,2},{7,3},{8,12},{9,13},{10,... | collective-permute-start | bytes 1572872 | tf_op jit(solution)/shard_map/ppermute | solution.py:449
  14.0 31.0 %collective-permute-start.5 = (bf16[256,1024]{1,0:T(8,128)(2,1)}, bf16[256,1024]{1,0:T(8,128)(2,1)}, u32[]{:S(2)}, u32[]{:S(2)}) collective-permute-start(bf16[256,1024]{1,0:T(8,128)(2,1)} %get-tuple-element.89.refs_6_), channel_id=1, source_target_pairs={{0,8},{1,9},{2,10},{3,11},{4,12},{5,13},{6,14},{7,15},{8,0},{9,1},... | collective-permute-start | bytes 1572872 | tf_op jit(solution)/shard_map/ppermute | solution.py:449
  21.1 64.9 %collective-permute-start = (bf16[256,4096]{1,0:T(8,128)(2,1)}, bf16[256,4096]{1,0:T(8,128)(2,1)S(1)}, u32[]{:S(2)}, u32[]{:S(2)}) collective-permute-start(bf16[256,4096]{1,0:T(8,128)(2,1)} %shard_map.219), channel_id=1, source_target_pairs={{0,1},{1,0},{2,3},{3,2},{4,5},{5,4},{6,7},{7,6},{8,9},{9,8},{10,11... | collective-permute-start | bytes 6291464 | tf_op jit(solution)/shard_map/ppermute | solution.py:449
  24.7 18.8 %collective-permute-start.6 = (bf16[256,1024]{1,0:T(8,128)(2,1)}, bf16[256,1024]{1,0:T(8,128)(2,1)}, u32[]{:S(2)}, u32[]{:S(2)}) collective-permute-start(bf16[256,1024]{1,0:T(8,128)(2,1)} %collective-permute-done.2.refs_8_), channel_id=1, source_target_pairs={{0,16},{16,0},{1,17},{17,1},{2,18},{18,2},{3,19},{19,3},{4,20},{20... | collective-permute-start | bytes 1572872 | tf_op jit(solution)/shard_map/ppermute | solution.py:452
  26.5 18.5 %collective-permute-start.3 = (bf16[16,1152]{1,0:T(8,128)(2,1)S(1)}, bf16[16,1152]{1,0:T(8,128)(2,1)S(1)}, u32[]{:S(2)}, u32[]{:S(2)}) collective-permute-start(bf16[16,1152]{1,0:T(8,128)(2,1)S(1)} %pad_maximum_fusion.3), channel_id=1, source_target_pairs={{0,2},{1,3},{2,0},{3,1},{4,6},{5,7},{6,4},{7,5},{8,10},{9,11},{10,... | collective-permute-start | bytes 110600 | tf_op jit(solution)/shard_map/ppermute | solution.py:449
  43.5 40.4 %collective-permute-start.1 = (bf16[256,1024]{1,0:T(8,128)(2,1)S(1)}, bf16[256,1024]{1,0:T(8,128)(2,1)}, u32[]{:S(2)}, u32[]{:S(2)}) collective-permute-start(bf16[256,1024]{1,0:T(8,128)(2,1)S(1)} %multiply_convert_fusion.refs_2_), channel_id=1, source_target_pairs={{0,1},{1,0},{2,3},{3,2},{4,5},{5,4},{6,7},{7,6},{8,9},{9,8},{10,11... | collective-permute-start | bytes 1572872 | tf_op jit(solution)/shard_map/ppermute | solution.py:449
  43.5 14.5 %collective-permute-start.8 = (bf16[256,1024]{1,0:T(8,128)(2,1)}, bf16[256,1024]{1,0:T(8,128)(2,1)S(1)}, u32[]{:S(2)}, u32[]{:S(2)}) collective-permute-start(bf16[256,1024]{1,0:T(8,128)(2,1)} %collective-permute-done.4.refs_10_), channel_id=1, source_target_pairs={{0,16},{16,0},{1,17},{17,1},{2,18},{18,2},{3,19},{19,3},{4,20},{20... | collective-permute-start | bytes 1572872 | tf_op jit(solution)/shard_map/ppermute | solution.py:452
  58.8 16.7 %collective-permute-start.9 = (bf16[64,1152]{1,0:T(8,128)(2,1)S(1)}, bf16[64,1152]{1,0:T(8,128)(2,1)S(1)}, u32[]{:S(2)}, u32[]{:S(2)}) collective-permute-start(bf16[64,1152]{1,0:T(8,128)(2,1)S(1)} %pad_maximum_fusion.1), channel_id=1, source_target_pairs={{0,8},{1,9},{2,10},{3,11},{4,12},{5,13},{6,14},{7,15},{8,0},{9,1},... | collective-permute-start | bytes 442376 | tf_op jit(solution)/shard_map/ppermute | solution.py:449
  61.1 18.4 %collective-permute-start.11 = (bf16[256,1024]{1,0:T(8,128)(2,1)}, bf16[256,1024]{1,0:T(8,128)(2,1)}, u32[]{:S(2)}, u32[]{:S(2)}) collective-permute-start(bf16[256,1024]{1,0:T(8,128)(2,1)} %collective-permute-done.4.refs_10_), channel_id=1, source_target_pairs={{0,2},{1,3},{2,0},{3,1},{4,6},{5,7},{6,4},{7,5},{8,10},{9,11},{10,... | collective-permute-start | bytes 1572872 | tf_op jit(solution)/shard_map/ppermute | solution.py:449
  76.9 20.5 %collective-permute-start.14 = (bf16[256,1024]{1,0:T(8,128)(2,1)}, bf16[256,1024]{1,0:T(8,128)(2,1)}, u32[]{:S(2)}, u32[]{:S(2)}) collective-permute-start(bf16[256,1024]{1,0:T(8,128)(2,1)} %collective-permute-done.5.refs_6_), channel_id=1, source_target_pairs={{0,4},{1,5},{2,6},{3,7},{4,0},{5,1},{6,2},{7,3},{8,12},{9,13},{10,... | collective-permute-start | bytes 1572872 | tf_op jit(solution)/shard_map/ppermute | solution.py:449
  79.5 13.7 %collective-permute-start.12 = (bf16[256,1024]{1,0:T(8,128)(2,1)}, bf16[256,1024]{1,0:T(8,128)(2,1)S(1)}, u32[]{:S(2)}, u32[]{:S(2)}) collective-permute-start(bf16[256,1024]{1,0:T(8,128)(2,1)} %collective-permute-done.5.refs_6_), channel_id=1, source_target_pairs={{0,2},{1,3},{2,0},{3,1},{4,6},{5,7},{6,4},{7,5},{8,10},{9,11},{10,... | collective-permute-start | bytes 1572872 | tf_op jit(solution)/shard_map/ppermute | solution.py:449
  79.8 13.7 %collective-permute-start.15 = (bf16[256,1024]{1,0:T(8,128)(2,1)}, bf16[256,1024]{1,0:T(8,128)(2,1)}, u32[]{:S(2)}, u32[]{:S(2)}) collective-permute-start(bf16[256,1024]{1,0:T(8,128)(2,1)} %collective-permute-done.11.refs_12_), channel_id=1, source_target_pairs={{0,16},{16,0},{1,17},{17,1},{2,18},{18,2},{3,19},{19,3},{4,20},{20... | collective-permute-start | bytes 1572872 | tf_op jit(solution)/shard_map/ppermute | solution.py:452
  93.2 24.1 %collective-permute-start.13 = (bf16[256,2048]{1,0:T(8,128)(2,1)}, bf16[256,2048]{1,0:T(8,128)(2,1)S(1)}, u32[]{:S(2)}, u32[]{:S(2)}) collective-permute-start(bf16[256,2048]{1,0:T(8,128)(2,1)} %shard_map.220), channel_id=1, source_target_pairs={{0,2},{1,3},{2,0},{3,1},{4,6},{5,7},{6,4},{7,5},{8,10},{9,11},{10,... | collective-permute-start | bytes 3145736 | tf_op jit(solution)/shard_map/ppermute | solution.py:449
  94.0 12.8 %collective-permute-start.16 = (bf16[256,1024]{1,0:T(8,128)(2,1)}, bf16[256,1024]{1,0:T(8,128)(2,1)S(1)}, u32[]{:S(2)}, u32[]{:S(2)}) collective-permute-start(bf16[256,1024]{1,0:T(8,128)(2,1)} %collective-permute-done.5.refs_6_), channel_id=1, source_target_pairs={{0,16},{16,0},{1,17},{17,1},{2,18},{18,2},{3,19},{19,3},{4,20},{20... | collective-permute-start | bytes 1572872 | tf_op jit(solution)/shard_map/ppermute | solution.py:452
  106.8 16.1 %collective-permute-start.17 = (bf16[256,1024]{1,0:T(8,128)(2,1)S(1)}, bf16[256,1024]{1,0:T(8,128)(2,1)}, u32[]{:S(2)}, u32[]{:S(2)}) collective-permute-start(bf16[256,1024]{1,0:T(8,128)(2,1)S(1)} %collective-permute-done.16.refs_7_), channel_id=1, source_target_pairs={{0,4},{1,5},{2,6},{3,7},{4,0},{5,1},{6,2},{7,3},{8,12},{9,13},{10,... | collective-permute-start | bytes 1572872 | tf_op jit(solution)/shard_map/ppermute | solution.py:449
  108.4 29.6 %collective-permute-start.19 = (bf16[256,1024]{1,0:T(8,128)(2,1)}, bf16[256,1024]{1,0:T(8,128)(2,1)}, u32[]{:S(2)}, u32[]{:S(2)}) collective-permute-start(bf16[256,1024]{1,0:T(8,128)(2,1)} %copy-done.26), channel_id=1, source_target_pairs={{0,16},{16,0},{1,17},{17,1},{2,18},{18,2},{3,19},{19,3},{4,20},{20... | collective-permute-start | bytes 1572872 | tf_op jit(solution)/shard_map/ppermute | solution.py:452
  122.4 15.5 %collective-permute-start.18 = (bf16[256,1024]{1,0:T(8,128)(2,1)}, bf16[256,1024]{1,0:T(8,128)(2,1)}, u32[]{:S(2)}, u32[]{:S(2)}) collective-permute-start(bf16[256,1024]{1,0:T(8,128)(2,1)} %collective-permute-done.14.refs_6_), channel_id=1, source_target_pairs={{0,2},{1,3},{2,0},{3,1},{4,6},{5,7},{6,4},{7,5},{8,10},{9,11},{10,... | collective-permute-start | bytes 1572872 | tf_op jit(solution)/shard_map/ppermute | solution.py:449
  123.0 16.5 %collective-permute-start.21 = (bf16[256,1024]{1,0:T(8,128)(2,1)}, bf16[256,1024]{1,0:T(8,128)(2,1)S(1)}, u32[]{:S(2)}, u32[]{:S(2)}) collective-permute-start(bf16[256,1024]{1,0:T(8,128)(2,1)} %get-tuple-element.59), channel_id=1, source_target_pairs={{0,4},{1,5},{2,6},{3,7},{4,0},{5,1},{6,2},{7,3},{8,12},{9,13},{10,... | collective-permute-start | bytes 1572872 | tf_op jit(solution)/shard_map/ppermute | solution.py:449
  125.1 11.1 %collective-permute-start.23 = (f32[4,2,16,1024]{3,2,1,0:T(8,128)S(1)}, f32[4,2,16,1024]{3,2,1,0:T(8,128)S(1)}, u32[]{:S(2)}, u32[]{:S(2)}) collective-permute-start(f32[4,2,16,1024]{3,2,1,0:T(8,128)S(1)} %dynamic-slice_bitcast_fusion), channel_id=1, source_target_pairs={{0,1},{1,0},{2,3},{3,2},{4,5},{5,4},{6,7},{7,6},{8,9},{9,8},{10,11... | collective-permute-start | bytes 1572872 | tf_op jit(solution)/shard_map/ppermute | solution.py:449
  138.0 24.5 %collective-permute-start.20 = (bf16[256,1024]{1,0:T(8,128)(2,1)}, bf16[256,1024]{1,0:T(8,128)(2,1)S(1)}, u32[]{:S(2)}, u32[]{:S(2)}) collective-permute-start(bf16[256,1024]{1,0:T(8,128)(2,1)} %collective-permute-done.18.refs_8_), channel_id=1, source_target_pairs={{0,16},{16,0},{1,17},{17,1},{2,18},{18,2},{3,19},{19,3},{4,20},{20... | collective-permute-start | bytes 1572872 | tf_op jit(solution)/shard_map/ppermute | solution.py:452
  139.6 15.9 %collective-permute-start.26 = (bf16[256,512]{1,0:T(8,128)(2,1)S(1)}, bf16[256,512]{1,0:T(8,128)(2,1)S(1)}, u32[]{:S(2)}, u32[]{:S(2)}) collective-permute-start(bf16[256,512]{1,0:T(8,128)(2,1)S(1)} %add_convert_fusion), channel_id=1, source_target_pairs={{0,8},{1,9},{2,10},{3,11},{4,12},{5,13},{6,14},{7,15},{8,0},{9,1},... | collective-permute-start | bytes 786440 | tf_op jit(solution)/shard_map/ppermute | solution.py:449
  152.1 10.3 %collective-permute-start.30 = (bf16[256,1024]{1,0:T(8,128)(2,1)}, bf16[256,1024]{1,0:T(8,128)(2,1)S(1)}, u32[]{:S(2)}, u32[]{:S(2)}) collective-permute-start(bf16[256,1024]{1,0:T(8,128)(2,1)} %get-tuple-element.72), channel_id=1, source_target_pairs={{0,1},{1,0},{2,3},{3,2},{4,5},{5,4},{6,7},{7,6},{8,9},{9,8},{10,11... | collective-permute-start | bytes 1572872 | tf_op jit(solution)/shard_map/ppermute | solution.py:449
  (43 other events, 396.2 us)
Sparse Core Ops, SparseCore 0:
  21.3 60.3 all-gather.1
